TPU v7x, 32 devices: a whole 2x2x4 slice. The times are simulated.
32 devices in a mesh: ctx: 8 (over y, x, core), head: 4 (over z).
Axes of the slice: x: 2, y: 2, z: 4, core: 2. Of those that a mesh axis runs over, the one named last changes fastest.
Arguments:
- attn_query: bfloat16 [4096, 32, 128], P('ctx', 'head'), may hold values from -6 to 6
- attn_key: bfloat16 [4096, 8, 128], P('ctx', 'head'), may hold values from -6 to 6
- attention_value: bfloat16 [4096, 8, 128], P('ctx', 'head'), may hold values from -6 to 6
- delta_query: bfloat16 [4096, 32, 128], P('ctx', 'head'), may hold values from -6 to 6
- delta_key: bfloat16 [4096, 32, 128], P('ctx', 'head'), may hold values from -6 to 6
- delta_value: bfloat16 [4096, 32, 128], P('ctx', 'head'), may hold values from -6 to 6
- log_decay: float32 [32, 4096], P('head', 'ctx'), may hold values from -0.8 to 0, as said below
- beta_gate: float32 [32, 4096], P('head', 'ctx'), may hold values from 0.1 to 0.9
Outputs:
- attn_out: bfloat16 [4096, 4096], P(('ctx', 'head'))
- delta_out: bfloat16 [4096, 4096], P(('ctx', 'head'))
Inputs may be any that keep to these rules, and one draw needn't show every extreme that they name: `log_decay`: each entry is the natural logarithm of a decay factor of one head at one token.
All inputs are finite; a program needn't handle non-finite values.
Results may differ from a plain program's by a relative error of at most 0.0045.
Values may be sent and summed in bfloat16 or wider, within the bound.
A program may use at most 128 MiB of HBM per device.

v0:
```python
import math

import jax
import jax.numpy as jnp
from jax import lax
from jax.sharding import PartitionSpec as P

WINDOW = 1024
SPAN = 64


norm_epsilon = 1e-06


def shifted(block, axis, distance):
    devices = range(lax.axis_size(axis))
    route = [(i - distance, i) for i in devices if i - distance in devices]
    return lax.ppermute(block, axis, route)


def product(form, left, right):
    return jnp.einsum(form, left, right, precision=lax.Precision.HIGHEST)


def normalize(tensor, scale_factor):
    widened = tensor.astype(jnp.float32)
    return (
        widened
        / jnp.sqrt(jnp.sum(widened * widened, axis=-1, keepdims=True) + norm_epsilon)
        * scale_factor
    )


def invert_unit(strict):
    span_len = strict.shape[-1]
    identity = jnp.eye(span_len, dtype=strict.dtype)
    inverse = identity - strict
    power_term = strict
    for level in range(1, max(1, (span_len - 1).bit_length())):
        power_term = product("hij,hjk->hik", power_term, power_term)
        inverse = inverse + product("hij,hjk->hik", inverse, power_term)
    return inverse


def prepare(query_unit, key_unit, beta_rows, log_rows):
    span_len = log_rows.shape[1]
    cumulative = jnp.cumsum(log_rows, axis=1)
    row_index = jnp.arange(span_len, dtype=jnp.int32)[:, None]
    col_index = jnp.arange(span_len, dtype=jnp.int32)[None, :]
    log_gap = cumulative[:, :, None] - cumulative[:, None, :]
    decay_ratio = jnp.exp(jnp.where(row_index >= col_index, log_gap, -jnp.inf))
    key_inner = product("hcd,hed->hce", key_unit, key_unit)
    strict = jnp.where(row_index > col_index, beta_rows[:, :, None] * decay_ratio * key_inner, 0.0)
    causal = product("hcd,hed->hce", query_unit, key_unit) * decay_ratio
    return (cumulative, invert_unit(strict), causal)


def advance(carried, query_unit, key_unit, value_rows, beta_rows, prepared):
    cumulative, inverse, causal = prepared
    leading = jnp.exp(cumulative)
    projected = product("hcd,hvd->hcv", key_unit, carried)
    right_side = beta_rows[:, :, None] * (value_rows - leading[:, :, None] * projected)
    weighted = product("hce,hev->hcv", inverse, right_side)
    result = leading[:, :, None] * product("hcd,hvd->hcv", query_unit, carried) + product(
        "hts,hsv->htv", causal, weighted
    )
    trailing = jnp.exp(cumulative[:, -1:] - cumulative)
    updated = jnp.exp(cumulative[:, -1])[:, None, None] * carried + product(
        "hsv,hsd->hvd", trailing[:, :, None] * weighted, key_unit
    )
    return (updated, result)


def to_spans(tensor, span_len):
    return tensor.reshape(
        tensor.shape[0] // span_len, span_len, tensor.shape[1], tensor.shape[2]
    ).transpose(0, 2, 1, 3)


def gate_spans(tensor, span_len):
    return tensor.reshape(tensor.shape[0], tensor.shape[1] // span_len, span_len).transpose(1, 0, 2)


def from_spans(tensor):
    return tensor.transpose(0, 2, 1, 3).reshape(
        tensor.shape[0] * tensor.shape[2], tensor.shape[1] * tensor.shape[3]
    )


def attend(query_tile_block, key_block, value_block, block_start, group_count):
    rows = query_tile_block.shape[0]
    head_dim = query_tile_block.shape[2]
    grouped = query_tile_block.reshape(rows, key_block.shape[1], group_count, head_dim)
    scores = jnp.einsum(
        "qgrd,kgd->grqk", grouped, key_block, preferred_element_type=jnp.float32
    ) * (1.0 / math.sqrt(head_dim))
    query_pos = block_start + jnp.arange(rows, dtype=jnp.int32)
    key_pos = block_start - WINDOW + jnp.arange(key_block.shape[0], dtype=jnp.int32)
    allowed = (
        (key_pos[None, :] <= query_pos[:, None])
        & (key_pos[None, :] > query_pos[:, None] - WINDOW)
        & (key_pos[None, :] >= 0)
    )
    scores = jnp.where(allowed, scores, -jnp.inf)
    row_max = jnp.max(scores, axis=-1, keepdims=True)
    unnormed = jnp.exp(scores - row_max)
    row_total = jnp.sum(unnormed, axis=-1)
    weights = unnormed.astype(jnp.bfloat16)
    mixed_out = jnp.einsum(
        "grqk,kgd->qgrd", weights, value_block, preferred_element_type=jnp.float32
    )
    mixed_out = mixed_out / jnp.transpose(row_total, (2, 0, 1))[..., None]
    return mixed_out.reshape(rows, -1).astype(jnp.bfloat16)


def local(
    attn_query, attn_key, attention_value, delta_query, delta_key, delta_value, log_decay, beta_gate
):
    tokens = attn_query.shape[0]
    head_dim = attn_query.shape[2]
    group_count = attn_query.shape[1] // attn_key.shape[1]
    reach_hops = -(-WINDOW // tokens)
    key_value = jnp.stack((attn_key, attention_value))
    pieces = []
    for distance in range(reach_hops, 0, -1):
        pieces.append(shifted(key_value, "ctx", distance))
    pieces.append(key_value)
    extended = jnp.concatenate(pieces, axis=1)
    anchor = lax.axis_index("ctx") * tokens
    blocks_out = attend(attn_query, extended[0], extended[1], anchor + 0, group_count)
    attn_out = lax.all_to_all(blocks_out, "head", split_axis=0, concat_axis=1, tiled=True)
    heads_dev = delta_query.shape[1]
    query_unit = normalize(delta_query, 1.0 / math.sqrt(head_dim))
    key_unit = normalize(delta_key, 1.0)
    inputs = (
        to_spans(query_unit, SPAN),
        to_spans(key_unit, SPAN),
        to_spans(delta_value.astype(jnp.float32), SPAN),
        gate_spans(beta_gate, SPAN),
        gate_spans(log_decay, SPAN),
    )
    zero_state = jnp.zeros((heads_dev, head_dim, head_dim), jnp.float32)
    identity = jnp.broadcast_to(
        jnp.eye(head_dim, dtype=jnp.float32), (heads_dev, head_dim, head_dim)
    )

    def paired_step(carried, span_inputs):
        source_state, transit = carried
        query_part, key_part, value_part, beta_part, log_part = span_inputs
        prepared = prepare(query_part, key_part, beta_part, log_part)
        source_next, local_result = advance(
            source_state, query_part, key_part, value_part, beta_part, prepared
        )
        transit_next, moved_query = advance(transit, query_part, key_part, 0.0, beta_part, prepared)
        return ((source_next, transit_next), (local_result, moved_query))

    (source_state, transit), (local_results, moved_queries) = lax.scan(
        paired_step, (zero_state, identity), inputs
    )

    def relay_step(turn, inbound):
        leaving = product("hij,hjk->hik", inbound, transit) + source_state
        return shifted(leaving, "ctx", 1)

    incoming = lax.fori_loop(0, lax.axis_size("ctx") - 1, relay_step, zero_state)
    result_spans = local_results + product("hvd,nhcd->nhcv", incoming, moved_queries)
    delta_local = from_spans(result_spans).astype(jnp.bfloat16)
    delta_out = lax.all_to_all(delta_local, "head", split_axis=0, concat_axis=1, tiled=True)
    return (attn_out, delta_out)


def solution(mesh):
    placed = (
        P("ctx", "head", None),
        P("ctx", "head", None),
        P("ctx", "head", None),
        P("ctx", "head", None),
        P("ctx", "head", None),
        P("ctx", "head", None),
        P("head", "ctx"),
        P("head", "ctx"),
    )
    return jax.shard_map(
        local,
        mesh=mesh,
        in_specs=placed,
        out_specs=(P(("ctx", "head"), None), P(("ctx", "head"), None)),
        check_vma=False,
    )
```

profile of v0, /device:TPU:3, one launch (start us, length us, event | category | flops | bytes accessed | tf_op | source)
XLA Modules:
  0.0 331.4 jit_solution(5027762453131299113)
XLA Ops:
  2.8 3.1 collective-permute-start.1
  6.0 4.0 %collective-permute-start.2 = (bf16[2,512,2,128]{3,1,2,0:T(8,128)(2,1)}, bf16[2,512,2,128]{3,1,2,0:T(8,128)(2,1)}, u32[]{:S(2)}, u32[]{:S(2)}) collective-permute-start(bf16[2,512,2,128]{3,1,2,0:T(8,128)(2,1)} %pad_maximum_fusion), channel_id=1, source_target_pairs={{0,4},{4,8},{8,12},{12,16},{16,20},{20,24},{24,28},{1,5},{5,9},{9,... | collective-permute-start | bytes 1572872 | tf_op jit(solution)/shard_map/ppermute | solution.py:18
  10.7 1.7 convert_divide_fusion.1
  13.2 1.8 fusion.32
  14.9 1.4 convert_bitcast_fusion
  16.6 154.4 %while.28 = (s32[]{:T(128)}, f32[8,128,128]{2,1,0:T(8,128)S(1)}, f32[8,128,128]{2,1,0:T(8,128)S(1)}, f32[8,8,64,128]{3,2,0,1:T(8,128)}, f32[8,8,64,128]{3,2,0,1:...) while((s32[]{:T(128)}, f32[8,128,128]{2,1,0:T(8,128)S(1)}, ...), condition=%wide.region_6.7_spmd.clone, body=%wide.region_4.6_spmd.clone.sunk | while | flops 1159839744 | bytes 16741753 | solution.py:157
  24.3 1.8 constant_dynamic-slice_fusion.10
  28.9 2.1 fusion.175
  43.6 1.8 constant_dynamic-slice_fusion.10
  48.2 2.1 fusion.175
  62.9 1.8 constant_dynamic-slice_fusion.10
  67.5 2.1 fusion.175
  82.1 1.8 constant_dynamic-slice_fusion.10
  86.8 2.1 fusion.175
  101.4 1.8 constant_dynamic-slice_fusion.10
  106.0 2.1 fusion.175
  120.7 1.8 constant_dynamic-slice_fusion.10
  125.3 2.1 fusion.175
  140.0 1.8 constant_dynamic-slice_fusion.10
  144.6 2.1 fusion.175
  159.3 1.8 constant_dynamic-slice_fusion.10
  163.9 2.1 fusion.175
  171.0 81.2 %while.27 = (s32[]{:T(128)}, f32[8,128,128]{2,1,0:T(8,128)S(1)}, f32[8,128,128]{2,1,0:T(8,128)S(1)}, f32[8,128,128]{2,1,0:T(8,128)S(1)}, s32[]{:T(128)}) while((s32[]{:T(128)}, f32[8,128,128]{2,1,0:T(8,128)S(1)}, f32[8,128,128]{2,1,0:T(8,128)S(1)}, f32[8,128,128]{2,1,0:T(8,128)S(1)}, s32[]{:T(128)}) %tuple.62), condition=%wide.region_8.9_spmd, body=%wide.region_7.8_spmd.sunk | while | flops 201457664 | bytes 4194405 | solution.py:165
  171.9 1.9 collective-permute-start
  173.9 6.1 %collective-permute-done = f32[8,128,128]{2,1,0:T(8,128)S(1)} collective-permute-done((f32[8,128,128]{2,1,0:T(8,128)S(1)}, f32[8,128,128]{2,1,0:T(8,128)S(1)}, u32[]{:S(2)}, u32[]{:S(2)}) %collective-permute-start) | collective-permute-done | bytes 524320 | tf_op jit(solution)/shard_map/while/body/eval_jaxpr/ppermute | solution.py:18
  180.6 5.3 %collective-permute-start = (f32[8,128,128]{2,1,0:T(8,128)S(1)}, f32[8,128,128]{2,1,0:T(8,128)S(1)}, u32[]{:S(2)}, u32[]{:S(2)}) collective-permute-start(f32[8,128,128]{2,1,0:T(8,128)S(1)} %convolution_add_fusion.18), channel_id=1, source_target_pairs={{0,4},{4,8},{8,12},{12,16},{16,20},{20,24},{24,28},{1,5},{5,9},{9,... | collective-permute-start | bytes 1572872 | tf_op jit(solution)/shard_map/while/body/eval_jaxpr/ppermute | solution.py:18
  185.9 6.1 %collective-permute-done = f32[8,128,128]{2,1,0:T(8,128)S(1)} collective-permute-done((f32[8,128,128]{2,1,0:T(8,128)S(1)}, f32[8,128,128]{2,1,0:T(8,128)S(1)}, u32[]{:S(2)}, u32[]{:S(2)}) %collective-permute-start) | collective-permute-done | bytes 524320 | tf_op jit(solution)/shard_map/while/body/eval_jaxpr/ppermute | solution.py:18
  192.7 5.3 %collective-permute-start = (f32[8,128,128]{2,1,0:T(8,128)S(1)}, f32[8,128,128]{2,1,0:T(8,128)S(1)}, u32[]{:S(2)}, u32[]{:S(2)}) collective-permute-start(f32[8,128,128]{2,1,0:T(8,128)S(1)} %convolution_add_fusion.18), channel_id=1, source_target_pairs={{0,4},{4,8},{8,12},{12,16},{16,20},{20,24},{24,28},{1,5},{5,9},{9,... | collective-permute-start | bytes 1572872 | tf_op jit(solution)/shard_map/while/body/eval_jaxpr/ppermute | solution.py:18
  198.0 6.1 %collective-permute-done = f32[8,128,128]{2,1,0:T(8,128)S(1)} collective-permute-done((f32[8,128,128]{2,1,0:T(8,128)S(1)}, f32[8,128,128]{2,1,0:T(8,128)S(1)}, u32[]{:S(2)}, u32[]{:S(2)}) %collective-permute-start) | collective-permute-done | bytes 524320 | tf_op jit(solution)/shard_map/while/body/eval_jaxpr/ppermute | solution.py:18
  204.7 5.3 %collective-permute-start = (f32[8,128,128]{2,1,0:T(8,128)S(1)}, f32[8,128,128]{2,1,0:T(8,128)S(1)}, u32[]{:S(2)}, u32[]{:S(2)}) collective-permute-start(f32[8,128,128]{2,1,0:T(8,128)S(1)} %convolution_add_fusion.18), channel_id=1, source_target_pairs={{0,4},{4,8},{8,12},{12,16},{16,20},{20,24},{24,28},{1,5},{5,9},{9,... | collective-permute-start | bytes 1572872 | tf_op jit(solution)/shard_map/while/body/eval_jaxpr/ppermute | solution.py:18
  210.0 6.1 %collective-permute-done = f32[8,128,128]{2,1,0:T(8,128)S(1)} collective-permute-done((f32[8,128,128]{2,1,0:T(8,128)S(1)}, f32[8,128,128]{2,1,0:T(8,128)S(1)}, u32[]{:S(2)}, u32[]{:S(2)}) %collective-permute-start) | collective-permute-done | bytes 524320 | tf_op jit(solution)/shard_map/while/body/eval_jaxpr/ppermute | solution.py:18
  216.8 5.3 %collective-permute-start = (f32[8,128,128]{2,1,0:T(8,128)S(1)}, f32[8,128,128]{2,1,0:T(8,128)S(1)}, u32[]{:S(2)}, u32[]{:S(2)}) collective-permute-start(f32[8,128,128]{2,1,0:T(8,128)S(1)} %convolution_add_fusion.18), channel_id=1, source_target_pairs={{0,4},{4,8},{8,12},{12,16},{16,20},{20,24},{24,28},{1,5},{5,9},{9,... | collective-permute-start | bytes 1572872 | tf_op jit(solution)/shard_map/while/body/eval_jaxpr/ppermute | solution.py:18
  222.1 6.1 %collective-permute-done = f32[8,128,128]{2,1,0:T(8,128)S(1)} collective-permute-done((f32[8,128,128]{2,1,0:T(8,128)S(1)}, f32[8,128,128]{2,1,0:T(8,128)S(1)}, u32[]{:S(2)}, u32[]{:S(2)}) %collective-permute-start) | collective-permute-done | bytes 524320 | tf_op jit(solution)/shard_map/while/body/eval_jaxpr/ppermute | solution.py:18
  228.8 5.3 %collective-permute-start = (f32[8,128,128]{2,1,0:T(8,128)S(1)}, f32[8,128,128]{2,1,0:T(8,128)S(1)}, u32[]{:S(2)}, u32[]{:S(2)}) collective-permute-start(f32[8,128,128]{2,1,0:T(8,128)S(1)} %convolution_add_fusion.18), channel_id=1, source_target_pairs={{0,4},{4,8},{8,12},{12,16},{16,20},{20,24},{24,28},{1,5},{5,9},{9,... | collective-permute-start | bytes 1572872 | tf_op jit(solution)/shard_map/while/body/eval_jaxpr/ppermute | solution.py:18
  234.1 6.1 %collective-permute-done = f32[8,128,128]{2,1,0:T(8,128)S(1)} collective-permute-done((f32[8,128,128]{2,1,0:T(8,128)S(1)}, f32[8,128,128]{2,1,0:T(8,128)S(1)}, u32[]{:S(2)}, u32[]{:S(2)}) %collective-permute-start) | collective-permute-done | bytes 524320 | tf_op jit(solution)/shard_map/while/body/eval_jaxpr/ppermute | solution.py:18
  240.9 5.3 %collective-permute-start = (f32[8,128,128]{2,1,0:T(8,128)S(1)}, f32[8,128,128]{2,1,0:T(8,128)S(1)}, u32[]{:S(2)}, u32[]{:S(2)}) collective-permute-start(f32[8,128,128]{2,1,0:T(8,128)S(1)} %convolution_add_fusion.18), channel_id=1, source_target_pairs={{0,4},{4,8},{8,12},{12,16},{16,20},{20,24},{24,28},{1,5},{5,9},{9,... | collective-permute-start | bytes 1572872 | tf_op jit(solution)/shard_map/while/body/eval_jaxpr/ppermute | solution.py:18
  246.2 6.1 %collective-permute-done = f32[8,128,128]{2,1,0:T(8,128)S(1)} collective-permute-done((f32[8,128,128]{2,1,0:T(8,128)S(1)}, f32[8,128,128]{2,1,0:T(8,128)S(1)}, u32[]{:S(2)}, u32[]{:S(2)}) %collective-permute-start) | collective-permute-done | bytes 524320 | tf_op jit(solution)/shard_map/while/body/eval_jaxpr/ppermute | solution.py:18
  252.3 4.2 %fusion.37 = bf16[8,64,8,128]{3,1,0,2:T(8,128)(2,1)S(1)} fusion(f32[8,8,64,128]{3,2,0,1:T(8,128)} %get-tuple-element.79, f32[8,8,64,128]{3,2,0,1:T(8,128)} %get-tuple-element.80, f32[8,128,128]{2,1,0:T(8,128)S(1)} %get-tuple-element.83), kind=kOutput, calls=%fused_computation.75 | convolution fusion | flops 806354944 | bytes 5767168 | tf_op jit(solution)/shard_map/hvd,nhcd->nhcv/dot_general | solution.py:22
  257.2 1.3 convert_element_type.45
  258.5 4.6 %all-to-all-start.1 = ((bf16[4,128,1024]{2,1,0:T(8,128)(2,1)}), bf16[4,128,1024]{2,1,0:T(8,128)(2,1)S(1)}, u32[]{:S(2)}, u32[]{:S(2)}) async-start(bf16[4,128,1024]{2,1,0:T(8,128)(2,1)} %convert_element_type.45), calls=%async_computation.1 | async-start | bytes 2097152 | tf_op jit(solution)/shard_map/all_to_all | solution.py:168
  264.3 1.3 maximum_maximum_fusion
  265.7 10.4 %fusion.26 = (f32[2,4,512]{2,1,0:T(4,128)S(1)}, f32[2,1536,512,4]{2,1,3,0:T(8,128)}) fusion(pred[512,1536]{0,1:T(8,128)(4,1)S(1)} %and_and_fusion, bf16[512,2,4,128]{3,2,1,0:T(4,128)(2,1)S(1)} %bitcast.229, bf16[2,1536,2,128]{3,1,2,0:T(8,128)(2,1)S(1)} %maximum_maximum_fusion), kind=kOutput, calls=%fused_computation.58 | convolution fusion | flops 1629483008 | bytes 27803648 | tf_op jit(solution)/shard_map/qgrd,kgd->grqk/dot_general | solution.py:94
  276.1 11.1 %fusion.24 = f32[2,4,512]{2,1,0:T(4,128)S(1)} fusion(f32[2,1536,512,4]{2,1,3,0:T(8,128)} %get-tuple-element.188, f32[2,4,512]{2,1,0:T(4,128)S(1)} %get-tuple-element.187, pred[512,1536]{0,1:T(8,128)(4,1)S(1)} %and_and_fusion), kind=kLoop, calls=%fused_computation.56 | loop fusion | flops 25161728 | bytes 25985024 | tf_op jit(solution)/shard_map/reduce_sum | solution.py:107
  287.2 12.6 %fusion.34 = bf16[512,2,4,128]{0,3,2,1:T(8,128)(2,1)} fusion(f32[2,1536,512,4]{2,1,3,0:T(8,128)} %get-tuple-element.188, f32[2,4,512]{2,1,0:T(4,128)S(1)} %get-tuple-element.187, pred[512,1536]{0,1:T(8,128)(4,1)S(1)} %and_and_fusion, f32[512,2,4]{0,2,1:T(4,128)S(1)} %bitcast.242, bf16[2,1536,2,128]{3,1,2,0:T(8,128)(2,1)S(1)} %maximum_maximum_fusion), kind=kOutput, calls=%fused_computation.73 | convolution fusion | flops 1636827136 | bytes 27820032 | tf_op jit(solution)/shard_map/grqk,kgd->qgrd/dot_general | solution.py:109
  299.8 1.3 convert_element_type.39
  302.3 4.5 %all-to-all-start = ((bf16[4,128,1024]{1,2,0:T(8,128)(2,1)}), bf16[4,128,1024]{1,2,0:T(8,128)(2,1)S(1)}, u32[]{:S(2)}, u32[]{:S(2)}) async-start(bf16[4,128,1024]{1,2,0:T(8,128)(2,1)} %copy.53), calls=%async_computation | async-start | bytes 2097152 | tf_op jit(solution)/shard_map/all_to_all | solution.py:131
  308.1 2.3 copy.64
  310.4 19.7 %all-to-all-done = bf16[4,128,1024]{1,2,0:T(8,128)(2,1)S(1)} async-done(((bf16[4,128,1024]{1,2,0:T(8,128)(2,1)}), bf16[4,128,1024]{1,2,0:T(8,128)(2,1)S(1)}, u32[]{:S(2)}, u32[]{:S(2)}) %all-to-all-start) | async-done | bytes 1048608 | tf_op jit(solution)/shard_map/all_to_all | solution.py:131
  (284 shorter events, 135.9 us)
Async XLA Ops:
  0.6 265.0 %copy-start = (bf16[512,8,128]{2,1,0:T(8,128)(2,1)S(1)}, bf16[512,8,128]{2,1,0:T(8,128)(2,1)}, u32[]{:S(2)}) copy-start(bf16[512,8,128]{2,1,0:T(8,128)(2,1)} %param.12) | copy-start | bytes 3145732
  0.6 9.4 %copy-start.1 = (bf16[512,8,128]{2,1,0:T(8,128)(2,1)S(1)}, bf16[512,8,128]{2,1,0:T(8,128)(2,1)}, u32[]{:S(2)}) copy-start(bf16[512,8,128]{2,1,0:T(8,128)(2,1)} %param.16) | copy-start | bytes 3145732
  1.9 8.0 %copy-start.3 = (bf16[1,512,2,128]{3,1,2,0:T(8,128)(2,1)}, bf16[1,512,2,128]{3,1,2,0:T(8,128)(2,1)S(1)}, u32[]{:S(2)}) copy-start(bf16[1,512,2,128]{3,1,2,0:T(8,128)(2,1)S(1)} %get-tuple-element.191) | copy-start | bytes 786436
  1.9 8.0 %copy-start.5 = (bf16[1,512,2,128]{3,1,2,0:T(8,128)(2,1)}, bf16[1,512,2,128]{3,1,2,0:T(8,128)(2,1)S(1)}, u32[]{:S(2)}) copy-start(bf16[1,512,2,128]{3,1,2,0:T(8,128)(2,1)S(1)} %get-tuple-element.192) | copy-start | bytes 786436
  2.8 261.5 %collective-permute-start.1 = (bf16[2,512,2,128]{3,1,2,0:T(8,128)(2,1)}, bf16[2,512,2,128]{3,1,2,0:T(8,128)(2,1)}, u32[]{:S(2)}, u32[]{:S(2)}) collective-permute-start(bf16[2,512,2,128]{3,1,2,0:T(8,128)(2,1)} %pad_maximum_fusion), channel_id=1, source_target_pairs={{0,8},{4,12},{8,16},{12,20},{16,24},{20,28},{1,9},{5,13},{9,17},{1... | collective-permute-start | bytes 1572872 | tf_op jit(solution)/shard_map/ppermute | solution.py:18
  6.0 258.4 %collective-permute-start.2 = (bf16[2,512,2,128]{3,1,2,0:T(8,128)(2,1)}, bf16[2,512,2,128]{3,1,2,0:T(8,128)(2,1)}, u32[]{:S(2)}, u32[]{:S(2)}) collective-permute-start(bf16[2,512,2,128]{3,1,2,0:T(8,128)(2,1)} %pad_maximum_fusion), channel_id=1, source_target_pairs={{0,4},{4,8},{8,12},{12,16},{16,20},{20,24},{24,28},{1,5},{5,9},{9,... | collective-permute-start | bytes 1572872 | tf_op jit(solution)/shard_map/ppermute | solution.py:18
  10.6 1.8 copy-start.2
  13.1 1.9 copy-start.7
  14.9 1.5 copy-start.8
  14.9 1.5 copy-start.9
  171.9 8.0 %collective-permute-start = (f32[8,128,128]{2,1,0:T(8,128)S(1)}, f32[8,128,128]{2,1,0:T(8,128)S(1)}, u32[]{:S(2)}, u32[]{:S(2)}) collective-permute-start(f32[8,128,128]{2,1,0:T(8,128)S(1)} %convolution_add_fusion.18), channel_id=1, source_target_pairs={{0,4},{4,8},{8,12},{12,16},{16,20},{20,24},{24,28},{1,5},{5,9},{9,... | collective-permute-start | bytes 1572872 | tf_op jit(solution)/shard_map/while/body/eval_jaxpr/ppermute | solution.py:18
  180.6 11.4 %collective-permute-start = (f32[8,128,128]{2,1,0:T(8,128)S(1)}, f32[8,128,128]{2,1,0:T(8,128)S(1)}, u32[]{:S(2)}, u32[]{:S(2)}) collective-permute-start(f32[8,128,128]{2,1,0:T(8,128)S(1)} %convolution_add_fusion.18), channel_id=1, source_target_pairs={{0,4},{4,8},{8,12},{12,16},{16,20},{20,24},{24,28},{1,5},{5,9},{9,... | collective-permute-start | bytes 1572872 | tf_op jit(solution)/shard_map/while/body/eval_jaxpr/ppermute | solution.py:18
  192.7 11.4 %collective-permute-start = (f32[8,128,128]{2,1,0:T(8,128)S(1)}, f32[8,128,128]{2,1,0:T(8,128)S(1)}, u32[]{:S(2)}, u32[]{:S(2)}) collective-permute-start(f32[8,128,128]{2,1,0:T(8,128)S(1)} %convolution_add_fusion.18), channel_id=1, source_target_pairs={{0,4},{4,8},{8,12},{12,16},{16,20},{20,24},{24,28},{1,5},{5,9},{9,... | collective-permute-start | bytes 1572872 | tf_op jit(solution)/shard_map/while/body/eval_jaxpr/ppermute | solution.py:18
  204.7 11.4 %collective-permute-start = (f32[8,128,128]{2,1,0:T(8,128)S(1)}, f32[8,128,128]{2,1,0:T(8,128)S(1)}, u32[]{:S(2)}, u32[]{:S(2)}) collective-permute-start(f32[8,128,128]{2,1,0:T(8,128)S(1)} %convolution_add_fusion.18), channel_id=1, source_target_pairs={{0,4},{4,8},{8,12},{12,16},{16,20},{20,24},{24,28},{1,5},{5,9},{9,... | collective-permute-start | bytes 1572872 | tf_op jit(solution)/shard_map/while/body/eval_jaxpr/ppermute | solution.py:18
  216.8 11.4 %collective-permute-start = (f32[8,128,128]{2,1,0:T(8,128)S(1)}, f32[8,128,128]{2,1,0:T(8,128)S(1)}, u32[]{:S(2)}, u32[]{:S(2)}) collective-permute-start(f32[8,128,128]{2,1,0:T(8,128)S(1)} %convolution_add_fusion.18), channel_id=1, source_target_pairs={{0,4},{4,8},{8,12},{12,16},{16,20},{20,24},{24,28},{1,5},{5,9},{9,... | collective-permute-start | bytes 1572872 | tf_op jit(solution)/shard_map/while/body/eval_jaxpr/ppermute | solution.py:18
  228.8 11.4 %collective-permute-start = (f32[8,128,128]{2,1,0:T(8,128)S(1)}, f32[8,128,128]{2,1,0:T(8,128)S(1)}, u32[]{:S(2)}, u32[]{:S(2)}) collective-permute-start(f32[8,128,128]{2,1,0:T(8,128)S(1)} %convolution_add_fusion.18), channel_id=1, source_target_pairs={{0,4},{4,8},{8,12},{12,16},{16,20},{20,24},{24,28},{1,5},{5,9},{9,... | collective-permute-start | bytes 1572872 | tf_op jit(solution)/shard_map/while/body/eval_jaxpr/ppermute | solution.py:18
  240.9 11.4 %collective-permute-start = (f32[8,128,128]{2,1,0:T(8,128)S(1)}, f32[8,128,128]{2,1,0:T(8,128)S(1)}, u32[]{:S(2)}, u32[]{:S(2)}) collective-permute-start(f32[8,128,128]{2,1,0:T(8,128)S(1)} %convolution_add_fusion.18), channel_id=1, source_target_pairs={{0,4},{4,8},{8,12},{12,16},{16,20},{20,24},{24,28},{1,5},{5,9},{9,... | collective-permute-start | bytes 1572872 | tf_op jit(solution)/shard_map/while/body/eval_jaxpr/ppermute | solution.py:18
  257.2 7.1 %copy-start.4 = (bf16[1,512,2,128]{3,1,2,0:T(8,128)(2,1)S(1)}, bf16[1,512,2,128]{3,1,2,0:T(8,128)(2,1)}, u32[]{:S(2)}) copy-start(bf16[1,512,2,128]{3,1,2,0:T(8,128)(2,1)} %copy-done.3) | copy-start | bytes 786436
  257.2 7.1 %copy-start.6 = (bf16[1,512,2,128]{3,1,2,0:T(8,128)(2,1)S(1)}, bf16[1,512,2,128]{3,1,2,0:T(8,128)(2,1)}, u32[]{:S(2)}) copy-start(bf16[1,512,2,128]{3,1,2,0:T(8,128)(2,1)} %copy-done.5) | copy-start | bytes 786436
  258.5 43.7 %all-to-all-start.1 = ((bf16[4,128,1024]{2,1,0:T(8,128)(2,1)}), bf16[4,128,1024]{2,1,0:T(8,128)(2,1)S(1)}, u32[]{:S(2)}, u32[]{:S(2)}) async-start(bf16[4,128,1024]{2,1,0:T(8,128)(2,1)} %convert_element_type.45), calls=%async_computation.1 | async-start | bytes 2097152 | tf_op jit(solution)/shard_map/all_to_all | solution.py:168
  302.3 27.8 %all-to-all-start = ((bf16[4,128,1024]{1,2,0:T(8,128)(2,1)}), bf16[4,128,1024]{1,2,0:T(8,128)(2,1)S(1)}, u32[]{:S(2)}, u32[]{:S(2)}) async-start(bf16[4,128,1024]{1,2,0:T(8,128)(2,1)} %copy.53), calls=%async_computation | async-start | bytes 2097152 | tf_op jit(solution)/shard_map/all_to_all | solution.py:131
where the time goes:
time: 333 us; the launch traced here: 331 us
  matrix products  158 us (47%)
  waiting for transfers between devices  62.4 us (19%)
  starting transfers between devices  49.8 us (15%)
  local copies, waits for them, and re-layouts  34.4 us (10%)
  other arithmetic  23.3 us (7%)
    dot_general x184, matrix products, product(): return jnp.einsum(form, left, right, precision=lax.Precision.HIGHEST)  135 us
    ppermute x9, waiting for transfers between devices, shifted(): return lax.ppermute(block, axis, route)  42.7 us
    ppermute x9, starting transfers between devices, shifted(): return lax.ppermute(block, axis, route)  40.7 us
    dynamic_slice x24, local copies, waits for them, and re-layouts, local(): lax.scan(paired_step, (zero_state, identity), inputs)  22.1 us
    all_to_all x1, waiting for transfers between devices, local(): lax.all_to_all(blocks_out, 'head', split_axis=0, concat_axis=1, tiled=True)  19.7 us
    dot_general x1, matrix products, attend(): jnp.einsum('grqk,kgd->qgrd', weights, value_block, preferred_element_type...  12.6 us
    reduce_sum x1, other arithmetic, attend(): row_total = jnp.sum(unnormed, axis=-1)  11.1 us
    dot_general x1, matrix products, attend(): jnp.einsum('qgrd,kgd->grqk', grouped, key_block, preferred_element_type=j...  10.4 us
  transfers between devices with their start and end apart: 11, of which 8 were waited for; matrix products, arithmetic and copies ran while one was open for 64% of the time, Pallas kernels for 0%

commit v1 on v0

v1 whole, which is shorter than its diff:
```python
import functools
import math

import jax
import jax.numpy as jnp
from jax import lax
from jax.experimental import pallas as pl
from jax.experimental.pallas import tpu as pltpu
from jax.sharding import PartitionSpec as P

WINDOW = 1024
CHUNK = 128
PAIR = 2
norm_epsilon = 1e-06
F32, BF16 = jnp.float32, jnp.bfloat16
VMEM_BYTES = 56 * 1024 * 1024


def dot(a, b):
    return lax.dot_general(a, b, (((1,), (0,)), ((), ())), preferred_element_type=F32)


def dot_nt(a, b):
    return lax.dot_general(a, b, (((1,), (1,)), ((), ())), preferred_element_type=F32)


def split(x):
    high = x.astype(BF16)
    return high, (x - high.astype(F32)).astype(BF16)


def dot_square(a, b):
    ah, al = split(a)
    bh, bl = split(b)
    right = jnp.concatenate((bh, bl), axis=1)
    both = dot(jnp.concatenate((ah, al), axis=1), jnp.concatenate((right, right), axis=0))
    width = b.shape[1]
    return both[:, :width] + both[:, width:]


def dot_wide(a, b):
    ah, al = split(a)
    bh, bl = split(b)
    return dot(jnp.concatenate((ah, al), axis=1), jnp.concatenate((bh, bh), axis=0)) + dot(ah, bl)


def row_cumsum(row, upper):
    a = row.astype(BF16)
    rest = row - a.astype(F32)
    b = rest.astype(BF16)
    c = (rest - b.astype(F32)).astype(BF16)
    return dot(a, upper) + (dot(b, upper) + dot(c, upper))


def delta_spans(parts, head_dim):
    size = CHUNK
    row = lax.broadcasted_iota(jnp.int32, (size, size), 0)
    col = lax.broadcasted_iota(jnp.int32, (size, size), 1)
    upper = (row <= col).astype(BF16)
    eye = (row == col).astype(F32)
    state = []
    for q, k, v, log_row, beta_row in parts:
        qb, kb = q.astype(BF16), k.astype(BF16)
        rk = lax.rsqrt(jnp.sum(k * k, axis=1, keepdims=True) + norm_epsilon)
        rq = lax.rsqrt(jnp.sum(q * q, axis=1, keepdims=True) + norm_epsilon) / math.sqrt(head_dim)
        g = row_cumsum(jnp.broadcast_to(log_row, (8, size)), upper)[0:1, :]
        g_row = jnp.broadcast_to(g, (size, size))
        g_col = g_row.T
        b_col = jnp.broadcast_to(beta_row, (size, size)).T
        rk_row = jnp.broadcast_to(rk, (size, size)).T
        ratio = jnp.exp(jnp.where(row >= col, g_col - g_row, -jnp.inf)) * rk_row
        strict = jnp.where(row > col, b_col * rk * ratio * dot_nt(kb, kb), 0.0)
        causal = rq * ratio * dot_nt(qb, kb)
        state.append((strict, causal, g_col, b_col, rk, rq, g))
    inverse = []
    first = (row // 2 == col // 2) & (row > col)
    for s in state:
        inverse.append(eye - jnp.where(first, s[0], 0.0))
    block = 2
    while block < size:
        mask = (row // (2 * block) == col // (2 * block)) & (row // block > col // block)
        half = [dot_square(t, jnp.where(mask, s[0], 0.0)) for t, s in zip(inverse, state)]
        inverse = [t - dot_square(x, t) for t, x in zip(inverse, half)]
        block *= 2
    out = []
    for (q, k, v, _, _), t, (strict, causal, g_col, b_col, rk, rq, g) in zip(parts, inverse, state):
        lead = jnp.exp(g_col)
        weighted = dot_wide(t, jnp.concatenate((b_col * lead * rk * k, b_col * v), axis=1))
        mixed = dot_wide(causal, weighted)
        queries = lead * rq * q - mixed[:, :head_dim]
        last = g[:, size - 1 : size]
        trail = jnp.exp(last - g_col) * rk
        th, tl = split(jnp.concatenate((trail, trail), axis=1) * weighted)
        kt = k.T.astype(BF16)
        written = dot(jnp.concatenate((kt, kt), axis=1), jnp.concatenate((th, tl), axis=0))
        out.append((queries, mixed[:, head_dim:], jnp.exp(last), written))
    return out


def compose(spans, head_dim):
    zeros = jnp.zeros((head_dim, head_dim), F32)
    r = lax.broadcasted_iota(jnp.int32, (head_dim, head_dim), 0)
    c = lax.broadcasted_iota(jnp.int32, (head_dim, head_dim), 1)
    eye = (r == c).astype(F32)
    carried, results = None, []
    for queries, mixed, keep, written in spans:
        if carried is None:
            results.append((queries, mixed))
            carried = jnp.concatenate((keep * eye - written[:, :head_dim], written[:, head_dim:]), axis=1)
        else:
            both = dot_wide(queries, carried)
            results.append((both[:, :head_dim], both[:, head_dim:] + mixed))
            step = dot_wide(written[:, :head_dim], carried)
            carried = keep * carried - step + jnp.concatenate((zeros, written[:, head_dim:]), axis=1)
    return results, carried


def delta_kernel(heads, tokens, q_ref, k_ref, v_ref, log_ref, beta_ref, moved_ref, local_ref, pair_ref, fq, fk, fv):
    head_dim = q_ref.shape[1]

    @pl.when(pl.program_id(0) == 0)
    def _():
        fq[...] = q_ref[...].astype(F32)
        fk[...] = k_ref[...].astype(F32)
        fv[...] = v_ref[...].astype(F32)

    count = tokens // CHUNK
    parts = []
    for j in range(PAIR):
        h = pl.program_id(0) * PAIR + j
        for c in range(count):
            rows = pl.ds(c * CHUNK * heads + h, CHUNK, stride=heads)
            lanes = slice(c * CHUNK, (c + 1) * CHUNK)
            pick = lax.broadcasted_iota(jnp.int32, (heads, CHUNK), 0) == h
            gates = [
                jnp.sum(jnp.where(pick, ref[:, lanes], 0.0), axis=0, keepdims=True) for ref in (log_ref, beta_ref)
            ]
            parts.append((fq[rows, :], fk[rows, :], fv[rows, :], *gates))
    spans = delta_spans(parts, head_dim)
    for j in range(PAIR):
        results, carried = compose(spans[j * count : (j + 1) * count], head_dim)
        for c, (moved, local_part) in enumerate(results):
            moved_ref[j, c * CHUNK : (c + 1) * CHUNK, :] = moved
            local_ref[j, c * CHUNK : (c + 1) * CHUNK, :] = local_part
        pair_ref[j] = carried.astype(pair_ref.dtype)


def delta_local(q, k, v, log_decay, beta):
    tokens, heads, d = q.shape
    flat = [x.reshape(tokens * heads, d) for x in (q, k, v)]
    full = pl.BlockSpec((tokens * heads, d), lambda i: (0, 0))
    gate = pl.BlockSpec((heads, tokens), lambda i: (0, 0))
    per_head = pl.BlockSpec((PAIR, tokens, d), lambda i: (i, 0, 0))
    return pl.pallas_call(
        functools.partial(delta_kernel, heads, tokens),
        grid=(heads // PAIR,),
        in_specs=[full, full, full, gate, gate],
        out_specs=[per_head, per_head, pl.BlockSpec((PAIR, d, 2 * d), lambda i: (i, 0, 0))],
        out_shape=[
            jax.ShapeDtypeStruct((heads, tokens, d), F32),
            jax.ShapeDtypeStruct((heads, tokens, d), F32),
            jax.ShapeDtypeStruct((heads, d, 2 * d), BF16),
        ],
        scratch_shapes=[pltpu.VMEM((tokens * heads, d), F32)] * 3,
        compiler_params=pltpu.CompilerParams(vmem_limit_bytes=VMEM_BYTES),
        cost_estimate=pl.CostEstimate(flops=10_000_000_000, bytes_accessed=8_000_000, transcendentals=0),
        name="delta_local",
    )(*flat, log_decay, beta)


def prefix_kernel(pair_ref, state_ref):
    n, d = pair_ref.shape[0], pair_ref.shape[1]
    state = jnp.zeros((d, d), F32)
    for i in range(n):
        state_ref[i] = state.astype(state_ref.dtype)
        if i < n - 1:
            sh, sl = split(state)
            move = pair_ref[i, :, :d]
            both = dot(jnp.concatenate((move, move), axis=1), jnp.concatenate((sh, sl), axis=0))
            state = both + pair_ref[i, :, d:].astype(F32)


def final_kernel(moved_ref, local_ref, state_ref, out_ref):
    sh = state_ref[0]
    mh, ml = split(moved_ref[0])
    both = dot(jnp.concatenate((mh, ml), axis=1), jnp.concatenate((sh, sh), axis=0))
    out_ref[...] = (both + local_ref[0]).astype(BF16)


def delta_final(moved, local_part, states):
    heads, tokens, d = moved.shape
    per_head = pl.BlockSpec((1, tokens, d), lambda h: (h, 0, 0))
    return pl.pallas_call(
        final_kernel,
        grid=(heads,),
        in_specs=[per_head, per_head, pl.BlockSpec((1, d, d), lambda h: (h, 0, 0))],
        out_specs=pl.BlockSpec((tokens, d), lambda h: (0, h)),
        out_shape=jax.ShapeDtypeStruct((tokens, heads * d), BF16),
        compiler_params=pltpu.CompilerParams(vmem_limit_bytes=VMEM_BYTES),
        cost_estimate=pl.CostEstimate(flops=2_000_000_000, bytes_accessed=6_000_000, transcendentals=0),
        name="delta_final",
    )(moved, local_part, states)


def incoming_states(pairs):
    heads, d = pairs.shape[0], pairs.shape[1]
    n = lax.axis_size("ctx")
    if n == heads:
        mine = lax.all_to_all(pairs, "ctx", split_axis=0, concat_axis=0, tiled=True)
        states = pl.pallas_call(
            prefix_kernel,
            out_shape=jax.ShapeDtypeStruct((n, d, d), BF16),
            cost_estimate=pl.CostEstimate(flops=500_000_000, bytes_accessed=800_000, transcendentals=0),
            name="prefix",
        )(mine)
        return lax.all_to_all(states, "ctx", split_axis=0, concat_axis=0, tiled=True)
    transit, source = pairs[:, :, :d].astype(F32), pairs[:, :, d:].astype(F32)

    def relay(turn, inbound):
        leaving = jnp.einsum("hij,hjk->hik", transit, inbound, precision=lax.Precision.HIGHEST) + source
        return lax.ppermute(leaving, "ctx", [(i, i + 1) for i in range(n - 1)])

    return lax.fori_loop(0, n - 1, relay, jnp.zeros((heads, d, d), F32)).astype(BF16)


ROWS = 128


def attend_kernel(heads, groups, tokens, q_ref, *refs):
    count = len(refs) - 5
    shards = count // 2
    key_refs, value_refs = refs[:shards], refs[shards:count]
    out_ref, fq, fkv, keys, values = refs[count:]
    d = q_ref.shape[1]
    reach = (shards - 1) * tokens
    ratio = heads // groups
    g = pl.program_id(0)

    @pl.when(g == 0)
    def _():
        fq[...] = q_ref[...].astype(F32)
        for s in range(shards):
            fkv[0, pl.ds(s * tokens * groups, tokens * groups), :] = key_refs[s][...].astype(F32)
            fkv[1, pl.ds(s * tokens * groups, tokens * groups), :] = value_refs[s][...].astype(F32)
        values[:, d:] = jnp.ones((values.shape[0], d), BF16)

    span = reach + tokens
    keys[...] = fkv[0, pl.ds(g, span, stride=groups), :].astype(BF16)
    values[:, :d] = fkv[1, pl.ds(g, span, stride=groups), :].astype(BF16)
    width = WINDOW + ROWS
    anchor = lax.axis_index("ctx") * tokens
    row = lax.broadcasted_iota(jnp.int32, (ROWS, ROWS), 0)
    col = lax.broadcasted_iota(jnp.int32, (ROWS, ROWS), 1)
    lane = lax.broadcasted_iota(jnp.int32, (1, width), 1)
    low = jnp.where(col > row, 0.0, -jnp.inf)
    high = jnp.where(col <= row, 0.0, -jnp.inf)
    factor = math.log2(math.e) / math.sqrt(d)
    for b in range(tokens // ROWS):
        start = reach - WINDOW + b * ROWS
        key_part = keys[start : start + width, :]
        value_part = values[start : start + width, :]
        exists = jnp.where(lane + (anchor - reach + start) >= 0, 0.0, -jnp.inf)
        for r in range(ratio):
            h = g * ratio + r
            q = fq[pl.ds(b * ROWS * heads + h, ROWS, stride=heads), :].astype(BF16)
            scores = dot_nt(q, key_part) + exists
            scores = jnp.concatenate(
                (scores[:, :ROWS] + low, scores[:, ROWS:WINDOW], scores[:, WINDOW:] + high), axis=1
            )
            top = jnp.max(scores, axis=1, keepdims=True)
            weights = jnp.exp2((scores - top) * factor).astype(BF16)
            mixed = dot(weights, value_part)
            out_ref[b * ROWS : (b + 1) * ROWS, r * d : (r + 1) * d] = (mixed[:, :d] / mixed[:, d:]).astype(BF16)


def attend(q, key_shards, value_shards):
    tokens, heads, d = q.shape
    groups = key_shards[0].shape[1]
    shards = len(key_shards)
    flat = [x.reshape(-1, d) for x in (q, *key_shards, *value_shards)]
    span = shards * tokens
    return pl.pallas_call(
        functools.partial(attend_kernel, heads, groups, tokens),
        grid=(groups,),
        in_specs=[pl.BlockSpec(x.shape, lambda g: (0, 0)) for x in flat],
        out_specs=pl.BlockSpec((tokens, heads // groups * d), lambda g: (0, g)),
        out_shape=jax.ShapeDtypeStruct((tokens, heads * d), BF16),
        scratch_shapes=[
            pltpu.VMEM((tokens * heads, d), F32),
            pltpu.VMEM((2, span * groups, d), F32),
            pltpu.VMEM((span, d), BF16),
            pltpu.VMEM((span, 2 * d), BF16),
        ],
        compiler_params=pltpu.CompilerParams(vmem_limit_bytes=VMEM_BYTES),
        cost_estimate=pl.CostEstimate(flops=8_000_000_000, bytes_accessed=4_000_000, transcendentals=5_000_000),
        name="attend",
    )(*flat)


def shifted(block, distance):
    n = lax.axis_size("ctx")
    return lax.ppermute(block, "ctx", [(i, i + distance) for i in range(n - distance)])


def local(
    attn_query, attn_key, attention_value, delta_query, delta_key, delta_value, log_decay, beta_gate
):
    tokens = attn_query.shape[0]
    hops = -(-WINDOW // tokens)
    keys = [shifted(attn_key, s) for s in range(hops, 0, -1)] + [attn_key]
    values = [shifted(attention_value, s) for s in range(hops, 0, -1)] + [attention_value]
    moved, local_part, pairs = delta_local(delta_query, delta_key, delta_value, log_decay, beta_gate)
    states = incoming_states(pairs)
    attn_local = attend(attn_query, keys, values)
    attn_out = lax.all_to_all(attn_local, "head", split_axis=0, concat_axis=1, tiled=True)
    delta = delta_final(moved, local_part, states)
    delta_out = lax.all_to_all(delta, "head", split_axis=0, concat_axis=1, tiled=True)
    return (attn_out, delta_out)


def solution(mesh):
    placed = (P("ctx", "head", None),) * 6 + (P("head", "ctx"),) * 2
    return jax.shard_map(
        local,
        mesh=mesh,
        in_specs=placed,
        out_specs=(P(("ctx", "head"), None), P(("ctx", "head"), None)),
        check_vma=False,
    )
```

time: 333 us -> 129 us (0.39)
  the two profiles are of different devices: /device:TPU:3 before, /device:TPU:2 now
where the time goes in v1:
time: 129 us; the launch traced here: 128 us
  waiting for transfers between devices  48.6 us (38%)
  Pallas kernels  46.9 us (36%)
  starting transfers between devices  28.4 us (22%)
  local copies, waits for them, and re-layouts  3.62 us (3%)
    pallas_call x1, Pallas kernels, delta_local(): pl.pallas_call(functools.partial(delta_kernel, heads, tokens), grid=(head...  27 us
    all_to_all x1, waiting for transfers between devices, local(): lax.all_to_all(delta, 'head', split_axis=0, concat_axis=1, tiled=True)  24.1 us
    all_to_all x1, waiting for transfers between devices, local(): lax.all_to_all(attn_local, 'head', split_axis=0, concat_axis=1, tiled=True)  18.5 us
    ppermute x4, starting transfers between devices, shifted(): lax.ppermute(block, 'ctx', [(i, i + distance) for i in range(n - distance)])  10.7 us
    pallas_call x1, Pallas kernels, attend(): pl.pallas_call(functools.partial(attend_kernel, heads, groups, tokens), g...  10.4 us
    pallas_call x1, Pallas kernels, delta_final(): pl.pallas_call(final_kernel, grid=(heads,), in_specs=[per_head, per_head,...  6.66 us
    ppermute x4, waiting for transfers between devices, shifted(): lax.ppermute(block, 'ctx', [(i, i + distance) for i in range(n - distance)])  6 us
    all_to_all x1, starting transfers between devices, incoming_states(): lax.all_to_all(states, 'ctx', split_axis=0, concat_axis=0, tiled=True)  5.08 us
  transfers between devices with their start and end apart: 8, of which 3 were waited for; matrix products, arithmetic and copies ran while one was open for 1% of the time, Pallas kernels for 16%

profile of v1, /device:TPU:2, one launch (start us, length us, event | category | flops | bytes accessed | tf_op | source)
XLA Modules:
  0.0 128.4 jit_solution(10686065449135877034)
XLA Ops:
  0.6 0.0 copy-start.2
  0.6 0.0 copy-start.3
  0.7 27.0 %delta_local.1 = (f32[8,512,128]{2,1,0:T(8,128)}, f32[8,512,128]{2,1,0:T(8,128)}, bf16[8,128,256]{2,1,0:T(8,128)(2,1)}) custom-call(bf16[4096,128]{1,0:T(8,128)(2,1)} %bitcast.24, bf16[4096,128]{1,0:T(8,128)(2,1)} %bitcast.25, bf16[4096,128]{1,0:T(8,128)(2,1)} %bitcast.26, f32[8,512]{1,0:T(8,128)} %log_ref.1, f32[8,512]{1,0:T(8,128)} %beta_ref.1), custom_call_target="tpu_custom_call" | custom-call | flops 10000000000 | bytes 8000000 | tf_op jit(solution)/shard_map/delta_local/pallas_call | solution.py:154
  27.7 4.3 %all-to-all-start.1 = ((bf16[8,128,256]{2,1,0:T(8,128)(2,1)}), bf16[8,128,256]{2,1,0:T(8,128)(2,1)S(1)}, u32[]{:S(2)}, u32[]{:S(2)}) async-start(bf16[8,128,256]{2,1,0:T(8,128)(2,1)} %get-tuple-element.7), calls=%async_computation.1 | async-start | bytes 1048576 | tf_op jit(solution)/shard_map/all_to_all | solution.py:209
  31.9 0.0 copy-done.2
  31.9 3.4 %collective-permute-start = (bf16[512,2,128]{2,1,0:T(2,128)(2,1)S(1)}, bf16[512,2,128]{2,1,0:T(2,128)(2,1)S(1)}, u32[]{:S(2)}, u32[]{:S(2)}) collective-permute-start(bf16[512,2,128]{2,1,0:T(2,128)(2,1)S(1)} %copy-done.2), channel_id=1, source_target_pairs={{0,8},{4,12},{8,16},{12,20},{16,24},{20,28},{1,9},{5,13},{9,17},{1... | collective-permute-start | bytes 786440 | tf_op jit(solution)/shard_map/ppermute | solution.py:302
  35.3 1.9 %collective-permute-start.1 = (bf16[512,2,128]{2,1,0:T(2,128)(2,1)S(1)}, bf16[512,2,128]{2,1,0:T(2,128)(2,1)S(1)}, u32[]{:S(2)}, u32[]{:S(2)}) collective-permute-start(bf16[512,2,128]{2,1,0:T(2,128)(2,1)S(1)} %copy-done.2), channel_id=1, source_target_pairs={{0,4},{4,8},{8,12},{12,16},{16,20},{20,24},{24,28},{1,5},{5,9},{9,... | collective-permute-start | bytes 786440 | tf_op jit(solution)/shard_map/ppermute | solution.py:302
  37.2 0.0 copy-done.3
  37.2 3.4 %collective-permute-start.2 = (bf16[512,2,128]{2,1,0:T(2,128)(2,1)S(1)}, bf16[512,2,128]{2,1,0:T(2,128)(2,1)S(1)}, u32[]{:S(2)}, u32[]{:S(2)}) collective-permute-start(bf16[512,2,128]{2,1,0:T(2,128)(2,1)S(1)} %copy-done.3), channel_id=1, source_target_pairs={{0,8},{4,12},{8,16},{12,20},{16,24},{20,28},{1,9},{5,13},{9,17},{1... | collective-permute-start | bytes 786440 | tf_op jit(solution)/shard_map/ppermute | solution.py:302
  40.6 2.0 %collective-permute-start.3 = (bf16[512,2,128]{2,1,0:T(2,128)(2,1)S(1)}, bf16[512,2,128]{2,1,0:T(2,128)(2,1)S(1)}, u32[]{:S(2)}, u32[]{:S(2)}) collective-permute-start(bf16[512,2,128]{2,1,0:T(2,128)(2,1)S(1)} %copy-done.3), channel_id=1, source_target_pairs={{0,4},{4,8},{8,12},{12,16},{16,20},{20,24},{24,28},{1,5},{5,9},{9,... | collective-permute-start | bytes 786440 | tf_op jit(solution)/shard_map/ppermute | solution.py:302
  42.6 0.0 all-to-all-done.1.pair_ref
  42.6 0.0 copy-start
  42.7 0.8 copy-done
  43.4 2.8 %prefix.1 = bf16[8,128,128]{2,1,0:T(8,128)(2,1)} custom-call(bf16[8,128,256]{2,1,0:T(8,128)(2,1)} %copy-done), custom_call_target="tpu_custom_call" | custom-call | flops 500000000 | bytes 800000 | tf_op jit(solution)/shard_map/prefix/pallas_call | solution.py:210
  46.3 5.1 %all-to-all-start.2 = ((bf16[8,128,128]{2,1,0:T(8,128)(2,1)}), bf16[8,128,128]{2,1,0:T(8,128)(2,1)S(1)}, u32[]{:S(2)}, u32[]{:S(2)}) async-start(bf16[8,128,128]{2,1,0:T(8,128)(2,1)} %prefix.1), calls=%async_computation.2 | async-start | bytes 524288 | tf_op jit(solution)/shard_map/all_to_all | solution.py:216
  51.4 0.0 collective-permute-done
  51.4 0.0 copy-start.4
  51.4 0.0 collective-permute-done.1
  51.4 0.0 copy-start.5
  51.4 0.0 collective-permute-done.2
  51.4 0.0 copy-start.6
  51.4 6.0 %collective-permute-done.3 = bf16[512,2,128]{2,1,0:T(2,128)(2,1)S(1)} collective-permute-done((bf16[512,2,128]{2,1,0:T(2,128)(2,1)S(1)}, bf16[512,2,128]{2,1,0:T(2,128)(2,1)S(1)}, u32[]{:S(2)}, u32[]{:S(2)}) %collective-permute-start.3) | collective-permute-done | bytes 262176 | tf_op jit(solution)/shard_map/ppermute | solution.py:302
  57.4 0.0 copy-start.7
  57.4 0.0 copy-done.4
  57.4 0.0 copy-done.5
  57.4 0.0 copy-done.6
  57.4 0.7 copy-done.7
  58.1 10.4 %attend.1 = bf16[512,1024]{1,0:T(8,128)(2,1)} custom-call(bf16[4096,128]{1,0:T(8,128)(2,1)} %bitcast.27, bf16[1024,128]{1,0:T(8,128)(2,1)} %bitcast.30, bf16[1024,128]{1,0:T(8,128)(2,1)} %bitcast.31, bf16[1024,128]{1,0:T(8,128)(2,1)} %bitcast.28, bf16[1024,128]{1,0:T(8,128)(2,1)} %bitcast.32, bf16[1024,128]{1,0:T(8,128)(2,1)} %bitcast.33, ...), custom_call_target="tpu_custom_call" | custom-call | flops 8000000000 | bytes 4000000 | tf_op jit(solution)/shard_map/attend/pallas_call | solution.py:282
  68.5 0.0 all-to-all-done.2.state_ref
  68.5 0.0 copy-start.1
  68.5 4.9 %all-to-all-start = ((bf16[4,128,1024]{2,1,0:T(8,128)(2,1)}), bf16[4,128,1024]{2,1,0:T(8,128)(2,1)S(1)}, u32[]{:S(2)}, u32[]{:S(2)}) async-start(bf16[4,128,1024]{2,1,0:T(8,128)(2,1)} %bitcast.20), calls=%async_computation | async-start | bytes 2097152 | tf_op jit(solution)/shard_map/all_to_all | solution.py:315
  73.4 0.0 copy-done.1
  73.4 6.7 %delta_final.1 = bf16[512,1024]{1,0:T(8,128)(2,1)} custom-call(f32[8,512,128]{2,1,0:T(8,128)} %get-tuple-element.5.moved_ref, f32[8,512,128]{2,1,0:T(8,128)} %get-tuple-element.6.local_ref, bf16[8,128,128]{2,1,0:T(8,128)(2,1)} %copy-done.1), custom_call_target="tpu_custom_call" | custom-call | flops 2000000000 | bytes 6000000 | tf_op jit(solution)/shard_map/delta_final/pallas_call | solution.py:193
  80.1 18.5 %all-to-all-done = bf16[4,128,1024]{2,1,0:T(8,128)(2,1)S(1)} async-done(((bf16[4,128,1024]{2,1,0:T(8,128)(2,1)}), bf16[4,128,1024]{2,1,0:T(8,128)(2,1)S(1)}, u32[]{:S(2)}, u32[]{:S(2)}) %all-to-all-start) | async-done | bytes 1048608 | tf_op jit(solution)/shard_map/all_to_all | solution.py:315
  98.6 3.5 %all-to-all-start.3 = ((bf16[4,128,1024]{2,1,0:T(8,128)(2,1)}), bf16[4,128,1024]{2,1,0:T(8,128)(2,1)S(1)}, u32[]{:S(2)}, u32[]{:S(2)}) async-start(bf16[4,128,1024]{2,1,0:T(8,128)(2,1)} %bitcast.22), calls=%async_computation.3 | async-start | bytes 2097152 | tf_op jit(solution)/shard_map/all_to_all | solution.py:317
  102.1 1.1 copy.12
  103.2 24.1 %all-to-all-done.3 = bf16[4,128,1024]{2,1,0:T(8,128)(2,1)S(1)} async-done(((bf16[4,128,1024]{2,1,0:T(8,128)(2,1)}), bf16[4,128,1024]{2,1,0:T(8,128)(2,1)S(1)}, u32[]{:S(2)}, u32[]{:S(2)}) %all-to-all-start.3) | async-done | bytes 1048608 | tf_op jit(solution)/shard_map/all_to_all | solution.py:317
  127.3 1.1 copy.13
Async XLA Ops:
  0.6 31.3 %copy-start.2 = (bf16[512,2,128]{2,1,0:T(2,128)(2,1)S(1)}, bf16[512,2,128]{2,1,0:T(2,128)(2,1)}, u32[]{:S(2)}) copy-start(bf16[512,2,128]{2,1,0:T(2,128)(2,1)} %param.9) | copy-start | bytes 786436
  0.6 36.6 %copy-start.3 = (bf16[512,2,128]{2,1,0:T(2,128)(2,1)S(1)}, bf16[512,2,128]{2,1,0:T(2,128)(2,1)}, u32[]{:S(2)}) copy-start(bf16[512,2,128]{2,1,0:T(2,128)(2,1)} %param.10) | copy-start | bytes 786436
  27.7 15.0 %all-to-all-start.1 = ((bf16[8,128,256]{2,1,0:T(8,128)(2,1)}), bf16[8,128,256]{2,1,0:T(8,128)(2,1)S(1)}, u32[]{:S(2)}, u32[]{:S(2)}) async-start(bf16[8,128,256]{2,1,0:T(8,128)(2,1)} %get-tuple-element.7), calls=%async_computation.1 | async-start | bytes 1048576 | tf_op jit(solution)/shard_map/all_to_all | solution.py:209
  31.9 19.4 %collective-permute-start = (bf16[512,2,128]{2,1,0:T(2,128)(2,1)S(1)}, bf16[512,2,128]{2,1,0:T(2,128)(2,1)S(1)}, u32[]{:S(2)}, u32[]{:S(2)}) collective-permute-start(bf16[512,2,128]{2,1,0:T(2,128)(2,1)S(1)} %copy-done.2), channel_id=1, source_target_pairs={{0,8},{4,12},{8,16},{12,20},{16,24},{20,28},{1,9},{5,13},{9,17},{1... | collective-permute-start | bytes 786440 | tf_op jit(solution)/shard_map/ppermute | solution.py:302
  35.3 16.1 %collective-permute-start.1 = (bf16[512,2,128]{2,1,0:T(2,128)(2,1)S(1)}, bf16[512,2,128]{2,1,0:T(2,128)(2,1)S(1)}, u32[]{:S(2)}, u32[]{:S(2)}) collective-permute-start(bf16[512,2,128]{2,1,0:T(2,128)(2,1)S(1)} %copy-done.2), channel_id=1, source_target_pairs={{0,4},{4,8},{8,12},{12,16},{16,20},{20,24},{24,28},{1,5},{5,9},{9,... | collective-permute-start | bytes 786440 | tf_op jit(solution)/shard_map/ppermute | solution.py:302
  37.2 14.2 %collective-permute-start.2 = (bf16[512,2,128]{2,1,0:T(2,128)(2,1)S(1)}, bf16[512,2,128]{2,1,0:T(2,128)(2,1)S(1)}, u32[]{:S(2)}, u32[]{:S(2)}) collective-permute-start(bf16[512,2,128]{2,1,0:T(2,128)(2,1)S(1)} %copy-done.3), channel_id=1, source_target_pairs={{0,8},{4,12},{8,16},{12,20},{16,24},{20,28},{1,9},{5,13},{9,17},{1... | collective-permute-start | bytes 786440 | tf_op jit(solution)/shard_map/ppermute | solution.py:302
  40.6 16.8 %collective-permute-start.3 = (bf16[512,2,128]{2,1,0:T(2,128)(2,1)S(1)}, bf16[512,2,128]{2,1,0:T(2,128)(2,1)S(1)}, u32[]{:S(2)}, u32[]{:S(2)}) collective-permute-start(bf16[512,2,128]{2,1,0:T(2,128)(2,1)S(1)} %copy-done.3), channel_id=1, source_target_pairs={{0,4},{4,8},{8,12},{12,16},{16,20},{20,24},{24,28},{1,5},{5,9},{9,... | collective-permute-start | bytes 786440 | tf_op jit(solution)/shard_map/ppermute | solution.py:302
  42.6 0.8 copy-start
  46.3 22.3 %all-to-all-start.2 = ((bf16[8,128,128]{2,1,0:T(8,128)(2,1)}), bf16[8,128,128]{2,1,0:T(8,128)(2,1)S(1)}, u32[]{:S(2)}, u32[]{:S(2)}) async-start(bf16[8,128,128]{2,1,0:T(8,128)(2,1)} %prefix.1), calls=%async_computation.2 | async-start | bytes 524288 | tf_op jit(solution)/shard_map/all_to_all | solution.py:216
  51.4 6.0 %copy-start.4 = (bf16[512,2,128]{2,1,0:T(2,128)(2,1)}, bf16[512,2,128]{2,1,0:T(2,128)(2,1)S(1)}, u32[]{:S(2)}) copy-start(bf16[512,2,128]{2,1,0:T(2,128)(2,1)S(1)} %collective-permute-done) | copy-start | bytes 786436
  51.4 6.0 %copy-start.5 = (bf16[512,2,128]{2,1,0:T(2,128)(2,1)}, bf16[512,2,128]{2,1,0:T(2,128)(2,1)S(1)}, u32[]{:S(2)}) copy-start(bf16[512,2,128]{2,1,0:T(2,128)(2,1)S(1)} %collective-permute-done.1) | copy-start | bytes 786436
  51.4 6.0 %copy-start.6 = (bf16[512,2,128]{2,1,0:T(2,128)(2,1)}, bf16[512,2,128]{2,1,0:T(2,128)(2,1)S(1)}, u32[]{:S(2)}) copy-start(bf16[512,2,128]{2,1,0:T(2,128)(2,1)S(1)} %collective-permute-done.2) | copy-start | bytes 786436
  57.4 0.7 copy-start.7
  68.5 4.9 %copy-start.1 = (bf16[8,128,128]{2,1,0:T(8,128)(2,1)}, bf16[8,128,128]{2,1,0:T(8,128)(2,1)S(1)}, u32[]{:S(2)}) copy-start(bf16[8,128,128]{2,1,0:T(8,128)(2,1)S(1)} %all-to-all-done.2.state_ref) | copy-start | bytes 786436
  68.5 30.0 %all-to-all-start = ((bf16[4,128,1024]{2,1,0:T(8,128)(2,1)}), bf16[4,128,1024]{2,1,0:T(8,128)(2,1)S(1)}, u32[]{:S(2)}, u32[]{:S(2)}) async-start(bf16[4,128,1024]{2,1,0:T(8,128)(2,1)} %bitcast.20), calls=%async_computation | async-start | bytes 2097152 | tf_op jit(solution)/shard_map/all_to_all | solution.py:315
  98.6 28.7 %all-to-all-start.3 = ((bf16[4,128,1024]{2,1,0:T(8,128)(2,1)}), bf16[4,128,1024]{2,1,0:T(8,128)(2,1)S(1)}, u32[]{:S(2)}, u32[]{:S(2)}) async-start(bf16[4,128,1024]{2,1,0:T(8,128)(2,1)} %bitcast.22), calls=%async_computation.3 | async-start | bytes 2097152 | tf_op jit(solution)/shard_map/all_to_all | solution.py:317

commit v2 on v1

--- a/solution.py
+++ b/solution.py
@@ -297,6 +297,195 @@
     )(*flat)
 
 
+def attend_rows(q, key_part, value_part, exists, low, high, factor):
+    d = q.shape[1]
+    scores = dot_nt(q, key_part) + exists
+    scores = jnp.concatenate((scores[:, :ROWS] + low, scores[:, ROWS:WINDOW], scores[:, WINDOW:] + high), axis=1)
+    top = jnp.max(scores, axis=1, keepdims=True)
+    weights = jnp.exp2((scores - top) * factor).astype(BF16)
+    mixed = dot(weights, value_part)
+    return (mixed[:, :d] / mixed[:, d:]).astype(BF16)
+
+
+def fused_kernel(n, heads, groups, tokens, shards, q_ref, *refs):
+    key_refs, value_refs = refs[:shards], refs[shards : 2 * shards]
+    moved_ref, local_ref, pair_ref, attn_ref, delta_ref = refs[2 * shards : 2 * shards + 5]
+    (fq, fkv, keys, values, moved, local_part, mine, states, incoming, attn_stage, delta_stage) = refs[2 * shards + 5 : 2 * shards + 16]
+    (load_sem, own_sem, attn_send, attn_recv, delta_send, delta_recv, go_send, go_recv, back_send, back_recv) = refs[2 * shards + 16 :]
+    d = q_ref.shape[1]
+    ratio = heads // groups
+    reach = (shards - 1) * tokens
+    span = reach + tokens
+    width = WINDOW + ROWS
+    team = tokens // ROWS
+    ctx, head = lax.axis_index("ctx"), lax.axis_index("head")
+
+    barrier = pltpu.get_barrier_semaphore()
+    for o in range(1, n):
+        pl.semaphore_signal(barrier, inc=1, device_id={"ctx": lax.rem(ctx + o, n)}, device_id_type=pl.DeviceIdType.MESH)
+    for o in range(1, team):
+        pl.semaphore_signal(barrier, inc=1, device_id={"head": lax.rem(head + o, team)}, device_id_type=pl.DeviceIdType.MESH)
+    loads = [
+        pltpu.make_async_copy(moved_ref, moved, load_sem.at[0]),
+        pltpu.make_async_copy(local_ref, local_part, load_sem.at[1]),
+    ]
+    for load in loads:
+        load.start()
+    fq[...] = q_ref[...].astype(F32)
+    for s in range(shards):
+        rows = pl.ds(s * tokens * groups, tokens * groups)
+        fkv[0, rows, :] = key_refs[s][...].astype(F32)
+        fkv[1, rows, :] = value_refs[s][...].astype(F32)
+    values[:, d:] = jnp.ones((span, d), BF16)
+    pl.semaphore_wait(barrier, n - 1 + team - 1)
+
+    def remote(src, dst, send, recv, where):
+        return pltpu.make_async_remote_copy(
+            src_ref=src, dst_ref=dst, send_sem=send, recv_sem=recv, device_id=where,
+            device_id_type=pl.DeviceIdType.MESH,
+        )
+
+    def go(o, slot):
+        to = lax.rem(ctx + o, n)
+        return remote(pair_ref.at[to], mine.at[slot], go_send.at[o - 1], go_recv.at[o - 1], {"ctx": to})
+
+    def back(o, slot):
+        to = lax.rem(ctx + o, n)
+        return remote(states.at[to], incoming.at[slot], back_send.at[o - 1], back_recv.at[o - 1], {"ctx": to})
+
+    for o in range(1, n):
+        go(o, ctx).start()
+    mine[ctx] = pair_ref[ctx]
+
+    anchor = ctx * tokens
+    row = lax.broadcasted_iota(jnp.int32, (ROWS, ROWS), 0)
+    col = lax.broadcasted_iota(jnp.int32, (ROWS, ROWS), 1)
+    lane = lax.broadcasted_iota(jnp.int32, (1, width), 1)
+    low = jnp.where(col > row, 0.0, -jnp.inf)
+    high = jnp.where(col <= row, 0.0, -jnp.inf)
+    factor = math.log2(math.e) / math.sqrt(d)
+    offsets = list(range(1, team)) + [0]
+
+    def attn_copy(g, o, owner):
+        to = lax.rem(head + o, team)
+        place = attn_ref.at[:, pl.ds(pl.multiple_of((owner * groups + g) * ratio * d, ratio * d), ratio * d)]
+        if o == 0:
+            return pltpu.make_async_copy(attn_stage.at[g, o], place, own_sem.at[g])
+        return remote(attn_stage.at[g, o], place, attn_send.at[g, o - 1], attn_recv.at[g, o - 1], {"head": to})
+
+    def one_group(g, _):
+        keys[...] = fkv[0, pl.ds(g, span, stride=groups), :].astype(BF16)
+        values[:, :d] = fkv[1, pl.ds(g, span, stride=groups), :].astype(BF16)
+        for o in offsets:
+            b = lax.rem(head + o, team)
+            start = pl.multiple_of(reach - WINDOW + b * ROWS, ROWS)
+            key_part = keys[pl.ds(start, width), :]
+            value_part = values[pl.ds(start, width), :]
+            exists = jnp.where(lane + (anchor - reach + start) >= 0, 0.0, -jnp.inf)
+            for r in range(ratio):
+                q = fq[pl.ds(b * ROWS * heads + g * ratio + r, ROWS, stride=heads), :].astype(BF16)
+                attn_stage[g, o, :, r * d : (r + 1) * d] = attend_rows(
+                    q, key_part, value_part, exists, low, high, factor
+                )
+            attn_copy(g, o, head).start()
+        return 0
+
+    lax.fori_loop(0, groups, one_group, 0)
+
+    for o in range(1, n):
+        go(o, lax.rem(ctx - o + n, n)).wait_recv()
+    state = jnp.zeros((d, d), F32)
+    for i in range(n):
+        states[i] = state.astype(BF16)
+        if i < n - 1:
+            sh, sl = split(state)
+            move = mine[i, :, :d]
+            both = dot(jnp.concatenate((move, move), axis=1), jnp.concatenate((sh, sl), axis=0))
+            state = both + mine[i, :, d:].astype(F32)
+    for o in range(1, n):
+        back(o, ctx).start()
+    incoming[ctx] = states[ctx]
+    for load in loads:
+        load.wait()
+    for o in range(1, n):
+        back(o, lax.rem(ctx - o + n, n)).wait_recv()
+
+    def delta_copy(o, owner):
+        to = lax.rem(head + o, team)
+        place = delta_ref.at[:, pl.ds(pl.multiple_of(owner * heads * d, heads * d), heads * d)]
+        if o == 0:
+            return pltpu.make_async_copy(delta_stage.at[o], place, own_sem.at[groups])
+        return remote(delta_stage.at[o], place, delta_send.at[o - 1], delta_recv.at[o - 1], {"head": to})
+
+    for o in offsets:
+        rows = pl.ds(pl.multiple_of(lax.rem(head + o, team) * ROWS, ROWS), ROWS)
+        for h in range(heads):
+            mh, ml = split(moved[h, rows, :])
+            sh = incoming[h]
+            both = dot(jnp.concatenate((mh, ml), axis=1), jnp.concatenate((sh, sh), axis=0))
+            delta_stage[o, :, h * d : (h + 1) * d] = (both + local_part[h, rows, :]).astype(BF16)
+        delta_copy(o, head).start()
+
+    for g in range(groups):
+        attn_copy(g, 0, head).wait()
+        for o in range(1, team):
+            attn_copy(g, o, head).wait_send()
+            attn_copy(g, o, lax.rem(head - o + team, team)).wait_recv()
+    delta_copy(0, head).wait()
+    for o in range(1, team):
+        delta_copy(o, head).wait_send()
+        delta_copy(o, lax.rem(head - o + team, team)).wait_recv()
+    for o in range(1, n):
+        go(o, ctx).wait_send()
+        back(o, ctx).wait_send()
+
+
+def fused(q, key_shards, value_shards, moved, local_part, pairs):
+    tokens, heads, d = q.shape
+    groups = key_shards[0].shape[1]
+    shards = len(key_shards)
+    n, team = lax.axis_size("ctx"), lax.axis_size("head")
+    flat = [x.reshape(-1, d) for x in (q, *key_shards, *value_shards)]
+    span = shards * tokens
+    vmem, anywhere = pl.BlockSpec(memory_space=pltpu.VMEM), pl.BlockSpec(memory_space=pl.ANY)
+    result = jax.ShapeDtypeStruct((ROWS, team * heads * d), BF16)
+    sems = pltpu.SemaphoreType.DMA
+    return pl.pallas_call(
+        functools.partial(fused_kernel, n, heads, groups, tokens, shards),
+        in_specs=[vmem] * len(flat) + [anywhere, anywhere, vmem],
+        out_specs=[anywhere, anywhere],
+        out_shape=[result, result],
+        scratch_shapes=[
+            pltpu.VMEM((tokens * heads, d), F32),
+            pltpu.VMEM((2, span * groups, d), F32),
+            pltpu.VMEM((span, d), BF16),
+            pltpu.VMEM((span, 2 * d), BF16),
+            pltpu.VMEM(moved.shape, F32),
+            pltpu.VMEM(local_part.shape, F32),
+            pltpu.VMEM((n, d, 2 * d), BF16),
+            pltpu.VMEM((n, d, d), BF16),
+            pltpu.VMEM((heads, d, d), BF16),
+            pltpu.VMEM((groups, team, ROWS, heads // groups * d), BF16),
+            pltpu.VMEM((team, ROWS, heads * d), BF16),
+            sems((2,)),
+            sems((groups + 1,)),
+            sems((groups, team - 1)),
+            sems((groups, team - 1)),
+            sems((team - 1,)),
+            sems((team - 1,)),
+            sems((n - 1,)),
+            sems((n - 1,)),
+            sems((n - 1,)),
+            sems((n - 1,)),
+        ],
+        compiler_params=pltpu.CompilerParams(
+            vmem_limit_bytes=VMEM_BYTES, collective_id=1, has_side_effects=True
+        ),
+        cost_estimate=pl.CostEstimate(flops=10_000_000_000, bytes_accessed=12_000_000, transcendentals=5_000_000),
+        name="attend_and_exchange",
+    )(*flat, moved, local_part, pairs)
+
+
 def shifted(block, distance):
     n = lax.axis_size("ctx")
     return lax.ppermute(block, "ctx", [(i, i + distance) for i in range(n - distance)])
@@ -310,6 +499,9 @@
     keys = [shifted(attn_key, s) for s in range(hops, 0, -1)] + [attn_key]
     values = [shifted(attention_value, s) for s in range(hops, 0, -1)] + [attention_value]
     moved, local_part, pairs = delta_local(delta_query, delta_key, delta_value, log_decay, beta_gate)
+    heads, team = attn_query.shape[1], lax.axis_size("head")
+    if lax.axis_size("ctx") == heads and tokens == team * ROWS:
+        return tuple(fused(attn_query, keys, values, moved, local_part, pairs))
     states = incoming_states(pairs)
     attn_local = attend(attn_query, keys, values)
     attn_out = lax.all_to_all(attn_local, "head", split_axis=0, concat_axis=1, tiled=True)

time: 129 us -> 97.4 us (0.76)
  the two profiles are of different devices: /device:TPU:2 before, /device:TPU:8 now
where the time goes in v2:
time: 97.4 us; the launch traced here: 96.9 us
  Pallas kernels  79.9 us (82%)
  starting transfers between devices  12 us (12%)
  local copies, waits for them, and re-layouts  4.24 us (4%)
    pallas_call x1, Pallas kernels, fused(): pl.pallas_call(functools.partial(fused_kernel, n, heads, groups, tokens,...  53 us
    pallas_call x1, Pallas kernels, delta_local(): pl.pallas_call(functools.partial(delta_kernel, heads, tokens), grid=(head...  27 us
    ppermute x4, starting transfers between devices, shifted(): lax.ppermute(block, 'ctx', [(i, i + distance) for i in range(n - distance)])  12 us
    unnamed x12, local copies, waits for them, and re-layouts  4.24 us
  transfers between devices with their start and end apart: 4, of which 0 were waited for; matrix products, arithmetic and copies ran while one was open for 0% of the time, Pallas kernels for 28%

profile of v2, /device:TPU:8, one launch (start us, length us, event | category | flops | bytes accessed | tf_op | source)
XLA Modules:
  0.0 96.9 jit_solution(17632384471820406410)
XLA Ops:
  0.6 3.4 %collective-permute-start = (bf16[512,2,128]{2,1,0:T(2,128)(2,1)}, bf16[512,2,128]{2,1,0:T(2,128)(2,1)S(1)}, u32[]{:S(2)}, u32[]{:S(2)}) collective-permute-start(bf16[512,2,128]{2,1,0:T(2,128)(2,1)} %param.9), channel_id=1, source_target_pairs={{0,8},{4,12},{8,16},{12,20},{16,24},{20,28},{1,9},{5,13},{9,17},{1... | collective-permute-start | bytes 786440 | tf_op jit(solution)/shard_map/ppermute | solution.py:491
  4.1 1.5 %collective-permute-start.1 = (bf16[512,2,128]{2,1,0:T(2,128)(2,1)}, bf16[512,2,128]{2,1,0:T(2,128)(2,1)S(1)}, u32[]{:S(2)}, u32[]{:S(2)}) collective-permute-start(bf16[512,2,128]{2,1,0:T(2,128)(2,1)} %param.9), channel_id=1, source_target_pairs={{0,4},{4,8},{8,12},{12,16},{16,20},{20,24},{24,28},{1,5},{5,9},{9,... | collective-permute-start | bytes 786440 | tf_op jit(solution)/shard_map/ppermute | solution.py:491
  5.5 3.8 %collective-permute-start.2 = (bf16[512,2,128]{2,1,0:T(2,128)(2,1)}, bf16[512,2,128]{2,1,0:T(2,128)(2,1)S(1)}, u32[]{:S(2)}, u32[]{:S(2)}) collective-permute-start(bf16[512,2,128]{2,1,0:T(2,128)(2,1)} %param.10), channel_id=1, source_target_pairs={{0,8},{4,12},{8,16},{12,20},{16,24},{20,28},{1,9},{5,13},{9,17},{1... | collective-permute-start | bytes 786440 | tf_op jit(solution)/shard_map/ppermute | solution.py:491
  9.4 3.2 %collective-permute-start.3 = (bf16[512,2,128]{2,1,0:T(2,128)(2,1)}, bf16[512,2,128]{2,1,0:T(2,128)(2,1)S(1)}, u32[]{:S(2)}, u32[]{:S(2)}) collective-permute-start(bf16[512,2,128]{2,1,0:T(2,128)(2,1)} %param.10), channel_id=1, source_target_pairs={{0,4},{4,8},{8,12},{12,16},{16,20},{20,24},{24,28},{1,5},{5,9},{9,... | collective-permute-start | bytes 786440 | tf_op jit(solution)/shard_map/ppermute | solution.py:491
  12.6 27.0 %delta_local.1 = (f32[8,512,128]{2,1,0:T(8,128)}, f32[8,512,128]{2,1,0:T(8,128)}, bf16[8,128,256]{2,1,0:T(8,128)(2,1)}) custom-call(bf16[4096,128]{1,0:T(8,128)(2,1)} %bitcast.10, bf16[4096,128]{1,0:T(8,128)(2,1)} %bitcast.11, bf16[4096,128]{1,0:T(8,128)(2,1)} %bitcast.12, f32[8,512]{1,0:T(8,128)} %log_ref.1, f32[8,512]{1,0:T(8,128)} %beta_ref.1), custom_call_target="tpu_custom_call" | custom-call | flops 10000000000 | bytes 8000000 | tf_op jit(solution)/shard_map/delta_local/pallas_call | solution.py:154
  39.6 0.0 collective-permute-done
  39.6 0.0 copy-start.1
  39.6 0.0 collective-permute-done.1
  39.6 0.0 copy-start.2
  39.6 0.0 collective-permute-done.2
  39.6 0.0 copy-start.3
  39.6 0.0 collective-permute-done.3
  39.6 0.0 copy-start.4
  39.7 0.6 copy-done.1
  40.3 0.1 copy-done.2
  40.4 0.1 copy-done.3
  40.5 0.1 copy-done.4
  40.5 53.0 %attend_and_exchange.1 = (bf16[128,4096]{1,0:T(8,128)(2,1)}, bf16[128,4096]{1,0:T(8,128)(2,1)}) custom-call(bf16[4096,128]{1,0:T(8,128)(2,1)} %bitcast.13, bf16[1024,128]{1,0:T(8,128)(2,1)} %bitcast.16, bf16[1024,128]{1,0:T(8,128)(2,1)} %bitcast.17, bf16[1024,128]{1,0:T(8,128)(2,1)} %bitcast.14, bf16[1024,128]{1,0:T(8,128)(2,1)} %bitcast.18, ...), custom_call_target="tpu_custom_call" | custom-call | flops 10000000000 | bytes 12000000 | tf_op jit(solution)/shard_map/attend_and_exchange/pallas_call | solution.py:453
  93.5 0.0 copy-start
  93.5 2.4 %copy.12 = bf16[128,4096]{1,0:T(8,128)(2,1)} copy(bf16[128,4096]{1,0:T(8,128)(2,1)} %get-tuple-element.10) | data formatting | bytes 2097152
  95.9 0.0 copy-done
  95.9 1.0 %copy.13 = bf16[128,4096]{1,0:T(8,128)(2,1)} copy(bf16[128,4096]{1,0:T(8,128)(2,1)S(1)} %copy-done) | data formatting | bytes 2097152
Async XLA Ops:
  0.6 39.0 %collective-permute-start = (bf16[512,2,128]{2,1,0:T(2,128)(2,1)}, bf16[512,2,128]{2,1,0:T(2,128)(2,1)S(1)}, u32[]{:S(2)}, u32[]{:S(2)}) collective-permute-start(bf16[512,2,128]{2,1,0:T(2,128)(2,1)} %param.9), channel_id=1, source_target_pairs={{0,8},{4,12},{8,16},{12,20},{16,24},{20,28},{1,9},{5,13},{9,17},{1... | collective-permute-start | bytes 786440 | tf_op jit(solution)/shard_map/ppermute | solution.py:491
  4.1 35.5 %collective-permute-start.1 = (bf16[512,2,128]{2,1,0:T(2,128)(2,1)}, bf16[512,2,128]{2,1,0:T(2,128)(2,1)S(1)}, u32[]{:S(2)}, u32[]{:S(2)}) collective-permute-start(bf16[512,2,128]{2,1,0:T(2,128)(2,1)} %param.9), channel_id=1, source_target_pairs={{0,4},{4,8},{8,12},{12,16},{16,20},{20,24},{24,28},{1,5},{5,9},{9,... | collective-permute-start | bytes 786440 | tf_op jit(solution)/shard_map/ppermute | solution.py:491
  5.5 34.1 %collective-permute-start.2 = (bf16[512,2,128]{2,1,0:T(2,128)(2,1)}, bf16[512,2,128]{2,1,0:T(2,128)(2,1)S(1)}, u32[]{:S(2)}, u32[]{:S(2)}) collective-permute-start(bf16[512,2,128]{2,1,0:T(2,128)(2,1)} %param.10), channel_id=1, source_target_pairs={{0,8},{4,12},{8,16},{12,20},{16,24},{20,28},{1,9},{5,13},{9,17},{1... | collective-permute-start | bytes 786440 | tf_op jit(solution)/shard_map/ppermute | solution.py:491
  9.4 30.2 %collective-permute-start.3 = (bf16[512,2,128]{2,1,0:T(2,128)(2,1)}, bf16[512,2,128]{2,1,0:T(2,128)(2,1)S(1)}, u32[]{:S(2)}, u32[]{:S(2)}) collective-permute-start(bf16[512,2,128]{2,1,0:T(2,128)(2,1)} %param.10), channel_id=1, source_target_pairs={{0,4},{4,8},{8,12},{12,16},{16,20},{20,24},{24,28},{1,5},{5,9},{9,... | collective-permute-start | bytes 786440 | tf_op jit(solution)/shard_map/ppermute | solution.py:491
  39.6 0.7 copy-start.1
  39.6 0.8 copy-start.2
  39.6 0.8 copy-start.3
  39.6 0.9 copy-start.4
  93.5 2.4 %copy-start = (bf16[128,4096]{1,0:T(8,128)(2,1)S(1)}, bf16[128,4096]{1,0:T(8,128)(2,1)}, u32[]{:S(2)}) copy-start(bf16[128,4096]{1,0:T(8,128)(2,1)} %get-tuple-element.11) | copy-start | bytes 3145732

commit v3 on v2

--- a/solution.py
+++ b/solution.py
@@ -307,11 +307,11 @@
     return (mixed[:, :d] / mixed[:, d:]).astype(BF16)
 
 
-def fused_kernel(n, heads, groups, tokens, shards, q_ref, *refs):
-    key_refs, value_refs = refs[:shards], refs[shards : 2 * shards]
-    moved_ref, local_ref, pair_ref, attn_ref, delta_ref = refs[2 * shards : 2 * shards + 5]
-    (fq, fkv, keys, values, moved, local_part, mine, states, incoming, attn_stage, delta_stage) = refs[2 * shards + 5 : 2 * shards + 16]
-    (load_sem, own_sem, attn_send, attn_recv, delta_send, delta_recv, go_send, go_recv, back_send, back_recv) = refs[2 * shards + 16 :]
+def fused_kernel(n, heads, groups, tokens, shards, *refs):
+    q_ref, key_ref, value_ref, dq_ref, dk_ref, dv_ref, log_ref, beta_ref, attn_ref, delta_ref = refs[:10]
+    halo, fq, fkv, keys, values, moved, local_part, pair_ref, mine, states, incoming, attn_stage, delta_stage = refs[10:23]
+    dq, dk, dv = refs[23:26]
+    halo_send, halo_recv, own_sem, attn_send, attn_recv, delta_send, delta_recv, go_send, go_recv, back_send, back_recv = refs[26:]
     d = q_ref.shape[1]
     ratio = heads // groups
     reach = (shards - 1) * tokens
@@ -325,18 +325,6 @@
         pl.semaphore_signal(barrier, inc=1, device_id={"ctx": lax.rem(ctx + o, n)}, device_id_type=pl.DeviceIdType.MESH)
     for o in range(1, team):
         pl.semaphore_signal(barrier, inc=1, device_id={"head": lax.rem(head + o, team)}, device_id_type=pl.DeviceIdType.MESH)
-    loads = [
-        pltpu.make_async_copy(moved_ref, moved, load_sem.at[0]),
-        pltpu.make_async_copy(local_ref, local_part, load_sem.at[1]),
-    ]
-    for load in loads:
-        load.start()
-    fq[...] = q_ref[...].astype(F32)
-    for s in range(shards):
-        rows = pl.ds(s * tokens * groups, tokens * groups)
-        fkv[0, rows, :] = key_refs[s][...].astype(F32)
-        fkv[1, rows, :] = value_refs[s][...].astype(F32)
-    values[:, d:] = jnp.ones((span, d), BF16)
     pl.semaphore_wait(barrier, n - 1 + team - 1)
 
     def remote(src, dst, send, recv, where):
@@ -353,9 +341,57 @@
         to = lax.rem(ctx + o, n)
         return remote(states.at[to], incoming.at[slot], back_send.at[o - 1], back_recv.at[o - 1], {"ctx": to})
 
-    for o in range(1, n):
-        go(o, ctx).start()
-    mine[ctx] = pair_ref[ctx]
+    def halo_copy(o, side):
+        source = (key_ref, value_ref)[side]
+        return remote(
+            source, halo.at[o - 1, side], halo_send.at[o - 1, side], halo_recv.at[o - 1, side],
+            {"ctx": lax.rem(ctx + o, n)},
+        )
+
+    hops = shards - 1
+    for o in range(1, shards):
+        for side in range(2):
+            halo_copy(o, side).start()
+    dq[...] = dq_ref[...].astype(F32)
+    dk[...] = dk_ref[...].astype(F32)
+    dv[...] = dv_ref[...].astype(F32)
+
+    def delta_pair(p, _):
+        count = tokens // CHUNK
+        parts = []
+        for j in range(PAIR):
+            h = p * PAIR + j
+            pick = lax.broadcasted_iota(jnp.int32, (heads, CHUNK), 0) == h
+            for c in range(count):
+                rows = pl.ds(c * CHUNK * heads + h, CHUNK, stride=heads)
+                lanes = slice(c * CHUNK, (c + 1) * CHUNK)
+                gates = [
+                    jnp.sum(jnp.where(pick, ref[:, lanes], 0.0), axis=0, keepdims=True)
+                    for ref in (log_ref, beta_ref)
+                ]
+                parts.append((dq[rows, :], dk[rows, :], dv[rows, :], *gates))
+        spans = delta_spans(parts, d)
+        for j in range(PAIR):
+            h = p * PAIR + j
+            results, carried = compose(spans[j * count : (j + 1) * count], d)
+            for c, (one, two) in enumerate(results):
+                moved[h, c * CHUNK : (c + 1) * CHUNK, :] = one
+                local_part[h, c * CHUNK : (c + 1) * CHUNK, :] = two
+            pair_ref[h] = carried.astype(BF16)
+        return 0
+
+    def attention():
+        fq[...] = q_ref[...].astype(F32)
+        own = pl.ds(hops * tokens * groups, tokens * groups)
+        fkv[0, own, :] = key_ref[...].astype(F32)
+        fkv[1, own, :] = value_ref[...].astype(F32)
+        values[:, d:] = jnp.ones((span, d), BF16)
+        for o in range(1, shards):
+            rows = pl.ds((hops - o) * tokens * groups, tokens * groups)
+            for side in range(2):
+                halo_copy(o, side).wait_recv()
+                fkv[side, rows, :] = halo[o - 1, side].astype(F32)
+        lax.fori_loop(0, groups, one_group, 0)
 
     anchor = ctx * tokens
     row = lax.broadcasted_iota(jnp.int32, (ROWS, ROWS), 0)
@@ -390,8 +426,18 @@
             attn_copy(g, o, head).start()
         return 0
 
-    lax.fori_loop(0, groups, one_group, 0)
-
+    def step(p, _):
+        @pl.when(p == 1)
+        def _():
+            attention()
+
+        return delta_pair(p, _)
+
+    lax.fori_loop(0, heads // PAIR, step, 0)
+
+    for o in range(1, n):
+        go(o, ctx).start()
+    mine[ctx] = pair_ref[ctx]
     for o in range(1, n):
         go(o, lax.rem(ctx - o + n, n)).wait_recv()
     state = jnp.zeros((d, d), F32)
@@ -405,8 +451,6 @@
     for o in range(1, n):
         back(o, ctx).start()
     incoming[ctx] = states[ctx]
-    for load in loads:
-        load.wait()
     for o in range(1, n):
         back(o, lax.rem(ctx - o + n, n)).wait_recv()
 
@@ -435,39 +479,48 @@
     for o in range(1, team):
         delta_copy(o, head).wait_send()
         delta_copy(o, lax.rem(head - o + team, team)).wait_recv()
+    for o in range(1, shards):
+        for side in range(2):
+            halo_copy(o, side).wait_send()
     for o in range(1, n):
         go(o, ctx).wait_send()
         back(o, ctx).wait_send()
 
 
-def fused(q, key_shards, value_shards, moved, local_part, pairs):
+def fused(q, k, v, delta_query, delta_key, delta_value, log_decay, beta):
     tokens, heads, d = q.shape
-    groups = key_shards[0].shape[1]
-    shards = len(key_shards)
+    groups = k.shape[1]
+    shards = -(-WINDOW // tokens) + 1
     n, team = lax.axis_size("ctx"), lax.axis_size("head")
-    flat = [x.reshape(-1, d) for x in (q, *key_shards, *value_shards)]
+    flat = [x.reshape(-1, d) for x in (q, k, v, delta_query, delta_key, delta_value)]
     span = shards * tokens
     vmem, anywhere = pl.BlockSpec(memory_space=pltpu.VMEM), pl.BlockSpec(memory_space=pl.ANY)
     result = jax.ShapeDtypeStruct((ROWS, team * heads * d), BF16)
     sems = pltpu.SemaphoreType.DMA
     return pl.pallas_call(
         functools.partial(fused_kernel, n, heads, groups, tokens, shards),
-        in_specs=[vmem] * len(flat) + [anywhere, anywhere, vmem],
+        in_specs=[vmem] * 8,
         out_specs=[anywhere, anywhere],
         out_shape=[result, result],
         scratch_shapes=[
+            pltpu.VMEM((shards - 1, 2, tokens * groups, d), BF16),
             pltpu.VMEM((tokens * heads, d), F32),
             pltpu.VMEM((2, span * groups, d), F32),
             pltpu.VMEM((span, d), BF16),
             pltpu.VMEM((span, 2 * d), BF16),
-            pltpu.VMEM(moved.shape, F32),
-            pltpu.VMEM(local_part.shape, F32),
+            pltpu.VMEM((heads, tokens, d), F32),
+            pltpu.VMEM((heads, tokens, d), F32),
+            pltpu.VMEM((heads, d, 2 * d), BF16),
             pltpu.VMEM((n, d, 2 * d), BF16),
             pltpu.VMEM((n, d, d), BF16),
             pltpu.VMEM((heads, d, d), BF16),
             pltpu.VMEM((groups, team, ROWS, heads // groups * d), BF16),
             pltpu.VMEM((team, ROWS, heads * d), BF16),
-            sems((2,)),
+            pltpu.VMEM((tokens * heads, d), F32),
+            pltpu.VMEM((tokens * heads, d), F32),
+            pltpu.VMEM((tokens * heads, d), F32),
+            sems((shards - 1, 2)),
+            sems((shards - 1, 2)),
             sems((groups + 1,)),
             sems((groups, team - 1)),
             sems((groups, team - 1)),
@@ -481,9 +534,9 @@
         compiler_params=pltpu.CompilerParams(
             vmem_limit_bytes=VMEM_BYTES, collective_id=1, has_side_effects=True
         ),
-        cost_estimate=pl.CostEstimate(flops=10_000_000_000, bytes_accessed=12_000_000, transcendentals=5_000_000),
-        name="attend_and_exchange",
-    )(*flat, moved, local_part, pairs)
+        cost_estimate=pl.CostEstimate(flops=20_000_000_000, bytes_accessed=12_000_000, transcendentals=5_000_000),
+        name="attend_and_delta",
+    )(*flat, log_decay, beta)
 
 
 def shifted(block, distance):
@@ -495,13 +548,18 @@
     attn_query, attn_key, attention_value, delta_query, delta_key, delta_value, log_decay, beta_gate
 ):
     tokens = attn_query.shape[0]
+    heads, team = attn_query.shape[1], lax.axis_size("head")
     hops = -(-WINDOW // tokens)
+    n = lax.axis_size("ctx")
+    if n == heads and tokens == team * ROWS and WINDOW % tokens == 0 and hops < n:
+        return tuple(
+            fused(
+                attn_query, attn_key, attention_value, delta_query, delta_key, delta_value, log_decay, beta_gate
+            )
+        )
     keys = [shifted(attn_key, s) for s in range(hops, 0, -1)] + [attn_key]
     values = [shifted(attention_value, s) for s in range(hops, 0, -1)] + [attention_value]
     moved, local_part, pairs = delta_local(delta_query, delta_key, delta_value, log_decay, beta_gate)
-    heads, team = attn_query.shape[1], lax.axis_size("head")
-    if lax.axis_size("ctx") == heads and tokens == team * ROWS:
-        return tuple(fused(attn_query, keys, values, moved, local_part, pairs))
     states = incoming_states(pairs)
     attn_local = attend(attn_query, keys, values)
     attn_out = lax.all_to_all(attn_local, "head", split_axis=0, concat_axis=1, tiled=True)

time: 97.4 us -> 92.8 us (0.953)
  starting transfers between devices: 12 us -> 0 us
  Pallas kernels: 79.9 us -> 88.6 us
    pallas_call x1, Pallas kernels: 53 us -> 88.6 us  [fused(): pl.pallas_call(functools.partial(fused_kernel, n, heads, groups, tokens,...]
    pallas_call x1 -> x0, Pallas kernels: 27 us -> none  [delta_local(): pl.pallas_call(functools.partial(delta_kernel, heads, tokens), grid=(head...]
    ppermute x4 -> x0, starting transfers between devices: 12 us -> none  [shifted(): lax.ppermute(block, 'ctx', [(i, i + distance) for i in range(n - distance)])]
    unnamed x12 -> x4, local copies, waits for them, and re-layouts: 4.24 us -> 3.35 us
  transfers between devices with their start and end apart: 4 -> 0, of which waited for: 0 -> 0; matrix products, arithmetic and copies ran while one was open for 0% -> 0% of each run, Pallas kernels for 28% -> 0%
where the time goes in v3:
time: 92.8 us; the launch traced here: 92.6 us
  Pallas kernels  88.6 us (95%)
  local copies, waits for them, and re-layouts  3.35 us (4%)
    pallas_call x1, Pallas kernels, fused(): pl.pallas_call(functools.partial(fused_kernel, n, heads, groups, tokens,...  88.6 us
    unnamed x4, local copies, waits for them, and re-layouts  3.35 us

profile of v3, /device:TPU:8, one launch (start us, length us, event | category | flops | bytes accessed | tf_op | source)
XLA Modules:
  0.0 92.6 jit_solution(16758588749983414831)
XLA Ops:
  0.6 88.6 %attend_and_delta.1 = (bf16[128,4096]{1,0:T(8,128)(2,1)}, bf16[128,4096]{1,0:T(8,128)(2,1)}) custom-call(bf16[4096,128]{1,0:T(8,128)(2,1)} %bitcast.6, bf16[1024,128]{1,0:T(8,128)(2,1)} %bitcast.10, bf16[1024,128]{1,0:T(8,128)(2,1)} %bitcast.11, bf16[4096,128]{1,0:T(8,128)(2,1)} %bitcast.7, bf16[4096,128]{1,0:T(8,128)(2,1)} %bitcast.8, ...), custom_call_target="tpu_custom_call" | custom-call | flops 20000000000 | bytes 12000000 | tf_op jit(solution)/shard_map/attend_and_delta/pallas_call | solution.py:500
  89.3 0.0 copy-start
  89.3 2.4 %copy.12 = bf16[128,4096]{1,0:T(8,128)(2,1)} copy(bf16[128,4096]{1,0:T(8,128)(2,1)} %get-tuple-element.4) | data formatting | bytes 2097152
  91.7 0.0 copy-done
  91.7 1.0 %copy.13 = bf16[128,4096]{1,0:T(8,128)(2,1)} copy(bf16[128,4096]{1,0:T(8,128)(2,1)S(1)} %copy-done) | data formatting | bytes 2097152
Async XLA Ops:
  89.3 2.4 %copy-start = (bf16[128,4096]{1,0:T(8,128)(2,1)S(1)}, bf16[128,4096]{1,0:T(8,128)(2,1)}, u32[]{:S(2)}) copy-start(bf16[128,4096]{1,0:T(8,128)(2,1)} %get-tuple-element.5) | copy-start | bytes 3145732

commit v4 on v3

--- a/solution.py
+++ b/solution.py
@@ -378,6 +378,15 @@
                 moved[h, c * CHUNK : (c + 1) * CHUNK, :] = one
                 local_part[h, c * CHUNK : (c + 1) * CHUNK, :] = two
             pair_ref[h] = carried.astype(BF16)
+
+            @pl.when(h == ctx)
+            def _():
+                mine[ctx] = pair_ref[ctx]
+
+            @pl.when(h != ctx)
+            def _():
+                go(lax.rem(h - ctx + n, n), ctx).start()
+
         return 0
 
     def attention():
@@ -431,13 +440,10 @@
         def _():
             attention()
 
-        return delta_pair(p, _)
+        return delta_pair(lax.rem(lax.div(ctx, PAIR) + 1 + p, heads // PAIR), _)
 
     lax.fori_loop(0, heads // PAIR, step, 0)
 
-    for o in range(1, n):
-        go(o, ctx).start()
-    mine[ctx] = pair_ref[ctx]
     for o in range(1, n):
         go(o, lax.rem(ctx - o + n, n)).wait_recv()
     state = jnp.zeros((d, d), F32)

time: 92.8 us -> 90.4 us (0.974)
  Pallas kernels: 88.6 us -> 86.3 us
    pallas_call x1, Pallas kernels: 88.6 us -> 86.3 us  [fused(): pl.pallas_call(functools.partial(fused_kernel, n, heads, groups, tokens,...]
where the time goes in v4:
time: 90.4 us; the launch traced here: 90.3 us
  Pallas kernels  86.3 us (95%)
  local copies, waits for them, and re-layouts  3.35 us (4%)
    pallas_call x1, Pallas kernels, fused(): pl.pallas_call(functools.partial(fused_kernel, n, heads, groups, tokens,...  86.3 us
    unnamed x4, local copies, waits for them, and re-layouts  3.35 us

profile of v4, /device:TPU:8, one launch (start us, length us, event | category | flops | bytes accessed | tf_op | source)
XLA Modules:
  0.0 90.3 jit_solution(11858653304846822189)
XLA Ops:
  0.6 86.3 %attend_and_delta.1 = (bf16[128,4096]{1,0:T(8,128)(2,1)}, bf16[128,4096]{1,0:T(8,128)(2,1)}) custom-call(bf16[4096,128]{1,0:T(8,128)(2,1)} %bitcast.6, bf16[1024,128]{1,0:T(8,128)(2,1)} %bitcast.10, bf16[1024,128]{1,0:T(8,128)(2,1)} %bitcast.11, bf16[4096,128]{1,0:T(8,128)(2,1)} %bitcast.7, bf16[4096,128]{1,0:T(8,128)(2,1)} %bitcast.8, ...), custom_call_target="tpu_custom_call" | custom-call | flops 20000000000 | bytes 12000000 | tf_op jit(solution)/shard_map/attend_and_delta/pallas_call | solution.py:506
  86.9 0.0 copy-start
  86.9 2.4 %copy.12 = bf16[128,4096]{1,0:T(8,128)(2,1)} copy(bf16[128,4096]{1,0:T(8,128)(2,1)} %get-tuple-element.4) | data formatting | bytes 2097152
  89.3 0.0 copy-done
  89.3 1.0 %copy.13 = bf16[128,4096]{1,0:T(8,128)(2,1)} copy(bf16[128,4096]{1,0:T(8,128)(2,1)S(1)} %copy-done) | data formatting | bytes 2097152
Async XLA Ops:
  86.9 2.4 %copy-start = (bf16[128,4096]{1,0:T(8,128)(2,1)S(1)}, bf16[128,4096]{1,0:T(8,128)(2,1)}, u32[]{:S(2)}) copy-start(bf16[128,4096]{1,0:T(8,128)(2,1)} %get-tuple-element.5) | copy-start | bytes 3145732
